TPU v7x, 128 devices: a whole 4x4x4 slice. The times are simulated.
128 devices in a mesh: chain: 8 (over x, z_lo), dp: 16 (over z_hi, y, core).
Axes of the slice: x: 4, y: 4, z: 4 (z_hi: 2, z_lo: 2; z = z_hi * 2 + z_lo), core: 2. Of those that a mesh axis runs over, the one named last changes fastest.
Arguments:
- tokens: bfloat16 [4, 1024, 3072], P(None, 'dp'), may hold values from -6 to 6
- cotangent: bfloat16 [4, 1024, 3072], P(None, 'dp'), may hold values from -6 to 6
- weights: bfloat16 [8, 3072, 3072], P('chain'), may hold values from -0.109375 to 0.109375
- gains: float32 [8, 3072], P('chain'), may hold values from 0.1 to 1.9
Outputs:
- weight_grad: bfloat16 [8, 3072, 3072], P('chain', 'dp')
- gain_grad: float32 [8, 3072], P('chain', 'dp')
All inputs are finite; a program needn't handle non-finite values.
Results may differ from a plain program's by a relative error of at most 0.029.
Values may be sent and summed in bfloat16 or wider, within the bound.
No kernel may reach another device: no remote copies, remote signals or barrier semaphores. Data moves between devices by JAX's collectives and lax.ppermute only.
A program may use at most 192 MiB of HBM per device.

v0:
```python
import jax
import jax.numpy as jnp
from jax import lax
from jax.sharding import PartitionSpec as P


def passed_along(block, axis, distance):
    devices = range(lax.axis_size(axis))
    route = [(i - distance, i) for i in devices if i - distance in devices]
    return lax.ppermute(block, axis, route)


def layer_parts(block_input, gain_row, weight):
    x_float = block_input.astype(jnp.float32)
    inv_rms = lax.rsqrt(jnp.mean(x_float * x_float, axis=-1, keepdims=True) + 1e-06)
    normed = x_float * inv_rms
    scaled = (normed * gain_row).astype(jnp.bfloat16)
    hidden = jnp.dot(scaled, weight, preferred_element_type=jnp.float32)
    return (x_float, inv_rms, normed, scaled, hidden)


def advance(block_input, gain_row, weight):
    x_float, inv_rms, normed, scaled, hidden = layer_parts(block_input, gain_row, weight)
    return (x_float + jax.nn.gelu(hidden)).astype(jnp.bfloat16)


def retreat(block_input, upstream, gain_row, weight):
    x_float, inv_rms, normed, scaled, hidden = layer_parts(block_input, gain_row, weight)
    grad_in = upstream.astype(jnp.float32)
    _, pullback = jax.vjp(jax.nn.gelu, hidden)
    grad_hidden = pullback(grad_in)[0].astype(jnp.bfloat16)
    grad_scaled = lax.dot_general(
        grad_hidden, weight, (((1,), (1,)), ((), ())), preferred_element_type=jnp.float32
    )
    gain_term = jnp.sum(grad_scaled * normed, axis=0)
    grad_normed = grad_scaled * gain_row
    grad_input = grad_in + inv_rms * (
        grad_normed - normed * jnp.mean(grad_normed * normed, axis=-1, keepdims=True)
    )
    return (scaled, grad_hidden, grad_input.astype(jnp.bfloat16), gain_term)


def on_device(tokens, cotangent, weights, gains):
    my_section = lax.axis_index("chain")
    chain_size = lax.axis_size("chain")
    micro_count, micro_rows, channels = tokens.shape
    weight = weights[0]
    gain_row = gains[0]
    moments = micro_count + chain_size - 1

    def forward_step(moment, carry):
        incoming, saved = carry
        micro_index = moment - my_section
        active = jnp.logical_and(micro_index >= 0, micro_index < micro_count)
        slot_index = jnp.clip(micro_index, 0, micro_count - 1)
        fresh = lax.dynamic_index_in_dim(tokens, slot_index, 0, keepdims=False)
        given = jnp.where(my_section == 0, fresh, incoming)
        previous = lax.dynamic_index_in_dim(saved, slot_index, 0, keepdims=False)
        saved = lax.dynamic_update_index_in_dim(
            saved, jnp.where(active, given, previous), slot_index, 0
        )
        output = lax.cond(
            active,
            lambda values: advance(values, gain_row, weight),
            lambda values: jnp.zeros_like(values),
            given,
        )
        incoming = passed_along(output, "chain", 1)
        return (incoming, saved)

    _, saved = lax.fori_loop(
        0, moments, forward_step, (jnp.zeros_like(tokens[0]), jnp.zeros_like(tokens))
    )
    held = saved

    def spare_step(operands):
        zero_rows = jnp.zeros_like(operands[0])
        return (zero_rows, zero_rows, zero_rows, jnp.zeros((channels,), jnp.float32))

    def backward_step(moment, carry):
        incoming, scaled_all, hidden_all, gain_total = carry
        micro_index = moment - (chain_size - 1 - my_section)
        active = jnp.logical_and(micro_index >= 0, micro_index < micro_count)
        slot_index = jnp.clip(micro_index, 0, micro_count - 1)
        given = jnp.where(
            my_section == chain_size - 1,
            lax.dynamic_index_in_dim(cotangent, slot_index, 0, keepdims=False),
            incoming,
        )
        block_input = lax.dynamic_index_in_dim(held, slot_index, 0, keepdims=False)
        scaled, grad_hidden, grad_input, gain_term = lax.cond(
            active,
            lambda operands: retreat(operands[0], operands[1], gain_row, weight),
            spare_step,
            (block_input, given),
        )
        old_scaled = lax.dynamic_index_in_dim(scaled_all, slot_index, 0, keepdims=False)
        old_hidden = lax.dynamic_index_in_dim(hidden_all, slot_index, 0, keepdims=False)
        scaled_all = lax.dynamic_update_index_in_dim(
            scaled_all, jnp.where(active, scaled, old_scaled), slot_index, 0
        )
        hidden_all = lax.dynamic_update_index_in_dim(
            hidden_all, jnp.where(active, grad_hidden, old_hidden), slot_index, 0
        )
        incoming = passed_along(grad_input, "chain", -1)
        return (incoming, scaled_all, hidden_all, gain_total + gain_term)

    start_carry = (
        jnp.zeros_like(tokens[0]),
        jnp.zeros_like(tokens),
        jnp.zeros_like(tokens),
        jnp.zeros((channels,), jnp.float32),
    )
    _, scaled_all, hidden_all, gain_total = lax.fori_loop(0, moments, backward_step, start_carry)
    span = micro_count * micro_rows
    scaled_flat = scaled_all.reshape(span, channels)
    hidden_flat = hidden_all.reshape(span, channels)
    gain_part = lax.optimization_barrier(gain_total.astype(jnp.bfloat16)).astype(jnp.float32)
    weight_part = lax.dot_general(
        scaled_flat, hidden_flat, (((0,), (0,)), ((), ())), preferred_element_type=jnp.float32
    )
    weight_part = lax.optimization_barrier(weight_part.astype(jnp.bfloat16)).astype(jnp.float32)
    weight_rows, gain_rows = (
        lax.psum_scatter(
            weight_part.astype(jnp.bfloat16), "dp", scatter_dimension=0, tiled=True
        ).astype(jnp.float32),
        lax.psum_scatter(
            gain_part.astype(jnp.bfloat16), "dp", scatter_dimension=0, tiled=True
        ).astype(jnp.float32),
    )
    return (weight_rows.astype(jnp.bfloat16)[None], gain_rows[None])


def solution(mesh):
    placed = (P(None, "dp", None), P(None, "dp", None), P("chain", None, None), P("chain", None))
    return jax.shard_map(
        on_device,
        mesh=mesh,
        in_specs=placed,
        out_specs=(P("chain", "dp", None), P("chain", "dp")),
        check_vma=False,
    )
```

profile of v0, /device:TPU:1, one launch (start us, length us, event | category | flops | bytes accessed | tf_op | source)
XLA Modules:
  0.0 796.9 jit_solution(3474081213919960468)
XLA Ops:
  7.9 193.6 %while.38 = (s32[]{:T(128)}, bf16[64,3072]{1,0:T(8,128)(2,1)S(1)}, bf16[4,64,3072]{2,1,0:T(8,128)(2,1)S(1)}, s32[]{:T(128)}, pred[]{:T(512)}, /*index=5*/bf16[4,...) while((s32[]{:T(128)}, bf16[64,3072]{1,0:T(8,128)(2,1)S(1)}, ...), condition=%wide.region_4.5_spmd, body=%wide.region_0.4_spmd.sunk | while | flops 1211891712 | bytes 24392964 | solution.py:71
  9.1 10.2 %conditional.5 = (bf16[64,3072]{1,0:T(8,128)(2,1)S(1)}) conditional(s32[]{:T(128)} %convert_element_type.111, () %tuple.101, (bf16[64,3072]{1,0:T(8,128)(2,1)S(1)}, f32[1,3072]{1,0:T(1,128)S(1)}, bf16[3072,3072]{1,0:T(8,128)(2,1)}) %tuple.102), branch_computations={%region_1.1_spmd, %region_2.3_spmd} | conditional | flops 1211498496 | bytes 20067336 | solution.py:62
  9.3 10.0 %fusion.3 = bf16[64,3072]{1,0:T(8,128)(2,1)S(1)} fusion(bf16[64,3072]{1,0:T(8,128)(2,1)S(1)} %get-tuple-element.441, bf16[3072,3072]{1,0:T(8,128)(2,1)} %get-tuple-element.443, f32[3072]{0:T(1024)S(1)} %bitcast.58, f32[64]{0:T(128)S(1)} %add_rsqrt_fusion), kind=kOutput, calls=%fused_computation.7 | convolution fusion | flops 1210908672 | bytes 19673344 | tf_op jit(solution)/shard_map/while/body/eval_jaxpr/cond/branch_1_fun/dot_general | solution.py:18
  20.6 7.2 collective-permute-done
  29.1 10.2 %conditional.5 = (bf16[64,3072]{1,0:T(8,128)(2,1)S(1)}) conditional(s32[]{:T(128)} %convert_element_type.111, () %tuple.101, (bf16[64,3072]{1,0:T(8,128)(2,1)S(1)}, f32[1,3072]{1,0:T(1,128)S(1)}, bf16[3072,3072]{1,0:T(8,128)(2,1)}) %tuple.102), branch_computations={%region_1.1_spmd, %region_2.3_spmd} | conditional | flops 1211498496 | bytes 20067336 | solution.py:62
  29.3 10.0 %fusion.3 = bf16[64,3072]{1,0:T(8,128)(2,1)S(1)} fusion(bf16[64,3072]{1,0:T(8,128)(2,1)S(1)} %get-tuple-element.441, bf16[3072,3072]{1,0:T(8,128)(2,1)} %get-tuple-element.443, f32[3072]{0:T(1024)S(1)} %bitcast.58, f32[64]{0:T(128)S(1)} %add_rsqrt_fusion), kind=kOutput, calls=%fused_computation.7 | convolution fusion | flops 1210908672 | bytes 19673344 | tf_op jit(solution)/shard_map/while/body/eval_jaxpr/cond/branch_1_fun/dot_general | solution.py:18
  43.4 6.3 collective-permute-done
  50.9 10.2 %conditional.5 = (bf16[64,3072]{1,0:T(8,128)(2,1)S(1)}) conditional(s32[]{:T(128)} %convert_element_type.111, () %tuple.101, (bf16[64,3072]{1,0:T(8,128)(2,1)S(1)}, f32[1,3072]{1,0:T(1,128)S(1)}, bf16[3072,3072]{1,0:T(8,128)(2,1)}) %tuple.102), branch_computations={%region_1.1_spmd, %region_2.3_spmd} | conditional | flops 1211498496 | bytes 20067336 | solution.py:62
  51.2 10.0 %fusion.3 = bf16[64,3072]{1,0:T(8,128)(2,1)S(1)} fusion(bf16[64,3072]{1,0:T(8,128)(2,1)S(1)} %get-tuple-element.441, bf16[3072,3072]{1,0:T(8,128)(2,1)} %get-tuple-element.443, f32[3072]{0:T(1024)S(1)} %bitcast.58, f32[64]{0:T(128)S(1)} %add_rsqrt_fusion), kind=kOutput, calls=%fused_computation.7 | convolution fusion | flops 1210908672 | bytes 19673344 | tf_op jit(solution)/shard_map/while/body/eval_jaxpr/cond/branch_1_fun/dot_general | solution.py:18
  65.3 5.4 collective-permute-done
  71.9 10.2 %conditional.5 = (bf16[64,3072]{1,0:T(8,128)(2,1)S(1)}) conditional(s32[]{:T(128)} %convert_element_type.111, () %tuple.101, (bf16[64,3072]{1,0:T(8,128)(2,1)S(1)}, f32[1,3072]{1,0:T(1,128)S(1)}, bf16[3072,3072]{1,0:T(8,128)(2,1)}) %tuple.102), branch_computations={%region_1.1_spmd, %region_2.3_spmd} | conditional | flops 1211498496 | bytes 20067336 | solution.py:62
  72.1 10.0 %fusion.3 = bf16[64,3072]{1,0:T(8,128)(2,1)S(1)} fusion(bf16[64,3072]{1,0:T(8,128)(2,1)S(1)} %get-tuple-element.441, bf16[3072,3072]{1,0:T(8,128)(2,1)} %get-tuple-element.443, f32[3072]{0:T(1024)S(1)} %bitcast.58, f32[64]{0:T(128)S(1)} %add_rsqrt_fusion), kind=kOutput, calls=%fused_computation.7 | convolution fusion | flops 1210908672 | bytes 19673344 | tf_op jit(solution)/shard_map/while/body/eval_jaxpr/cond/branch_1_fun/dot_general | solution.py:18
  86.2 4.7 collective-permute-done
  92.2 14.5 %collective-permute-start = (bf16[64,3072]{1,0:T(8,128)(2,1)S(1)}, bf16[64,3072]{1,0:T(8,128)(2,1)S(1)}, u32[]{:S(2)}, u32[]{:S(2)}) collective-permute-start(bf16[64,3072]{1,0:T(8,128)(2,1)S(1)} %get-tuple-element.792), channel_id=1, source_target_pairs={{0,16},{16,32},{32,48},{48,64},{64,80},{80,96},{96,112},{1,17},{17... | collective-permute-start | bytes 1179656 | tf_op jit(solution)/shard_map/while/body/eval_jaxpr/ppermute | solution.py:10
  106.7 4.7 collective-permute-done
  112.6 5.1 collective-permute-start
  117.7 4.7 collective-permute-done
  123.7 14.9 %collective-permute-start = (bf16[64,3072]{1,0:T(8,128)(2,1)S(1)}, bf16[64,3072]{1,0:T(8,128)(2,1)S(1)}, u32[]{:S(2)}, u32[]{:S(2)}) collective-permute-start(bf16[64,3072]{1,0:T(8,128)(2,1)S(1)} %get-tuple-element.792), channel_id=1, source_target_pairs={{0,16},{16,32},{32,48},{48,64},{64,80},{80,96},{96,112},{1,17},{17... | collective-permute-start | bytes 1179656 | tf_op jit(solution)/shard_map/while/body/eval_jaxpr/ppermute | solution.py:10
  144.5 4.7 collective-permute-start
  149.2 5.2 collective-permute-done
  155.7 10.7 %collective-permute-start = (bf16[64,3072]{1,0:T(8,128)(2,1)S(1)}, bf16[64,3072]{1,0:T(8,128)(2,1)S(1)}, u32[]{:S(2)}, u32[]{:S(2)}) collective-permute-start(bf16[64,3072]{1,0:T(8,128)(2,1)S(1)} %get-tuple-element.792), channel_id=1, source_target_pairs={{0,16},{16,32},{32,48},{48,64},{64,80},{80,96},{96,112},{1,17},{17... | collective-permute-start | bytes 1179656 | tf_op jit(solution)/shard_map/while/body/eval_jaxpr/ppermute | solution.py:10
  172.4 7.5 collective-permute-start
  179.9 7.7 collective-permute-done
  188.9 7.1 collective-permute-start
  196.0 5.5 collective-permute-done
  204.2 390.2 %while.39 = (s32[]{:T(128)}, bf16[64,3072]{1,0:T(8,128)(2,1)S(1)}, bf16[4,64,3072]{2,1,0:T(8,128)(2,1)}, bf16[4,64,3072]{2,1,0:T(8,128)(2,1)}, f32[3072]{0:T(102...) while((s32[]{:T(128)}, bf16[64,3072]{1,0:T(8,128)(2,1)S(1)}, ...), condition=%wide.region_11.12_spmd.clone, body=%wide.region_5.11_spmd.clone.sunk | while | flops 2425359360 | bytes 56319456 | solution.py:114
  211.4 10.2 %collective-permute-done.1 = bf16[64,3072]{1,0:T(8,128)(2,1)S(1)} collective-permute-done((bf16[64,3072]{1,0:T(8,128)(2,1)}, bf16[64,3072]{1,0:T(8,128)(2,1)S(1)}, u32[]{:S(2)}, u32[]{:S(2)}) %collective-permute-start.1) | collective-permute-done | bytes 393248 | tf_op jit(solution)/shard_map/while/body/eval_jaxpr/ppermute | solution.py:10
  228.8 8.2 %collective-permute-done.1 = bf16[64,3072]{1,0:T(8,128)(2,1)S(1)} collective-permute-done((bf16[64,3072]{1,0:T(8,128)(2,1)}, bf16[64,3072]{1,0:T(8,128)(2,1)S(1)}, u32[]{:S(2)}, u32[]{:S(2)}) %collective-permute-start.1) | collective-permute-done | bytes 393248 | tf_op jit(solution)/shard_map/while/body/eval_jaxpr/ppermute | solution.py:10
  244.2 14.6 %collective-permute-done.1 = bf16[64,3072]{1,0:T(8,128)(2,1)S(1)} collective-permute-done((bf16[64,3072]{1,0:T(8,128)(2,1)}, bf16[64,3072]{1,0:T(8,128)(2,1)S(1)}, u32[]{:S(2)}, u32[]{:S(2)}) %collective-permute-start.1) | collective-permute-done | bytes 393248 | tf_op jit(solution)/shard_map/while/body/eval_jaxpr/ppermute | solution.py:10
  266.0 8.7 %collective-permute-done.1 = bf16[64,3072]{1,0:T(8,128)(2,1)S(1)} collective-permute-done((bf16[64,3072]{1,0:T(8,128)(2,1)}, bf16[64,3072]{1,0:T(8,128)(2,1)S(1)}, u32[]{:S(2)}, u32[]{:S(2)}) %collective-permute-start.1) | collective-permute-done | bytes 393248 | tf_op jit(solution)/shard_map/while/body/eval_jaxpr/ppermute | solution.py:10
  281.9 10.3 %collective-permute-done.1 = bf16[64,3072]{1,0:T(8,128)(2,1)S(1)} collective-permute-done((bf16[64,3072]{1,0:T(8,128)(2,1)}, bf16[64,3072]{1,0:T(8,128)(2,1)S(1)}, u32[]{:S(2)}, u32[]{:S(2)}) %collective-permute-start.1) | collective-permute-done | bytes 393248 | tf_op jit(solution)/shard_map/while/body/eval_jaxpr/ppermute | solution.py:10
  299.4 8.6 %collective-permute-done.1 = bf16[64,3072]{1,0:T(8,128)(2,1)S(1)} collective-permute-done((bf16[64,3072]{1,0:T(8,128)(2,1)}, bf16[64,3072]{1,0:T(8,128)(2,1)S(1)}, u32[]{:S(2)}, u32[]{:S(2)}) %collective-permute-start.1) | collective-permute-done | bytes 393248 | tf_op jit(solution)/shard_map/while/body/eval_jaxpr/ppermute | solution.py:10
  315.2 145.6 %collective-permute-done.1 = bf16[64,3072]{1,0:T(8,128)(2,1)S(1)} collective-permute-done((bf16[64,3072]{1,0:T(8,128)(2,1)}, bf16[64,3072]{1,0:T(8,128)(2,1)S(1)}, u32[]{:S(2)}, u32[]{:S(2)}) %collective-permute-start.1) | collective-permute-done | bytes 393248 | tf_op jit(solution)/shard_map/while/body/eval_jaxpr/ppermute | solution.py:10
  460.8 24.0 %conditional.6 = (bf16[64,3072]{1,0:T(8,128)(2,1)S(1)}, bf16[64,3072]{1,0:T(8,128)(2,1)S(1)}, bf16[64,3072]{1,0:T(8,128)(2,1)}, f32[3072]{0:T(1024)}) conditional(s32[]{:T(128)} %convert_element_type.112, () %tuple.105, (bf16[4,64,3072]{2,1,0:T(8,128)(2,1)S(1)}, s32[]{:T(128)}, f32[1,3072]{1,0:T(1,128)S(1)}, pred[]{:T(512)}, ...), branch_computations={%region_6.6_spmd, %region_7.10_spmd} | conditional | flops 2424960000 | bytes 50776740 | solution.py:91
  461.2 10.3 %fusion.33 = bf16[64,3072]{1,0:T(8,128)(2,1)S(1)} fusion(bf16[64,3072]{1,0:T(8,128)(2,1)S(1)} %get-tuple-element.458, bf16[4,64,3072]{2,1,0:T(8,128)(2,1)} %get-tuple-element.457, s32[]{:T(128)} %get-tuple-element.454, pred[]{:T(512)} %get-tuple-element.456, bf16[64,3072]{1,0:T(8,128)(2,1)S(1)} %fusion.21, bf16[3072,3072]{1,0:T(8,128)(2,1)} %get-tuple-element.459), kind=kOutput, calls=%fused_computation.46 | convolution fusion | flops 1212284928 | bytes 20447236 | tf_op jit(solution)/shard_map/while/body/eval_jaxpr/cond/branch_1_fun/dot_general | solution.py:18
  471.5 10.5 %fusion.25 = (f32[3072]{0:T(1024)}, f32[64]{0:T(128)}, f32[64,3072]{1,0:T(8,128)S(1)}) fusion(f32[64]{0:T(128)S(1)} %add_rsqrt_fusion.1, bf16[4,64,3072]{2,1,0:T(8,128)(2,1)S(1)} %get-tuple-element.453, s32[]{:T(128)} %get-tuple-element.454, f32[3072]{0:T(1024)S(1)} %bitcast.60, bf16[64,3072]{1,0:T(8,128)(2,1)S(1)} %fusion.33, ...), kind=kOutput, calls=%fused_computation.38 | convolution fusion | flops 1209332736 | bytes 20472324 | tf_op jit(solution)/shard_map/while/body/eval_jaxpr/cond/branch_1_fun/dot_general | solution.py:32
  494.4 24.0 %conditional.6 = (bf16[64,3072]{1,0:T(8,128)(2,1)S(1)}, bf16[64,3072]{1,0:T(8,128)(2,1)S(1)}, bf16[64,3072]{1,0:T(8,128)(2,1)}, f32[3072]{0:T(1024)}) conditional(s32[]{:T(128)} %convert_element_type.112, () %tuple.105, (bf16[4,64,3072]{2,1,0:T(8,128)(2,1)S(1)}, s32[]{:T(128)}, f32[1,3072]{1,0:T(1,128)S(1)}, pred[]{:T(512)}, ...), branch_computations={%region_6.6_spmd, %region_7.10_spmd} | conditional | flops 2424960000 | bytes 50776740 | solution.py:91
  494.8 10.3 %fusion.33 = bf16[64,3072]{1,0:T(8,128)(2,1)S(1)} fusion(bf16[64,3072]{1,0:T(8,128)(2,1)S(1)} %get-tuple-element.458, bf16[4,64,3072]{2,1,0:T(8,128)(2,1)} %get-tuple-element.457, s32[]{:T(128)} %get-tuple-element.454, pred[]{:T(512)} %get-tuple-element.456, bf16[64,3072]{1,0:T(8,128)(2,1)S(1)} %fusion.21, bf16[3072,3072]{1,0:T(8,128)(2,1)} %get-tuple-element.459), kind=kOutput, calls=%fused_computation.46 | convolution fusion | flops 1212284928 | bytes 20447236 | tf_op jit(solution)/shard_map/while/body/eval_jaxpr/cond/branch_1_fun/dot_general | solution.py:18
  505.2 10.5 %fusion.25 = (f32[3072]{0:T(1024)}, f32[64]{0:T(128)}, f32[64,3072]{1,0:T(8,128)S(1)}) fusion(f32[64]{0:T(128)S(1)} %add_rsqrt_fusion.1, bf16[4,64,3072]{2,1,0:T(8,128)(2,1)S(1)} %get-tuple-element.453, s32[]{:T(128)} %get-tuple-element.454, f32[3072]{0:T(1024)S(1)} %bitcast.60, bf16[64,3072]{1,0:T(8,128)(2,1)S(1)} %fusion.33, ...), kind=kOutput, calls=%fused_computation.38 | convolution fusion | flops 1209332736 | bytes 20472324 | tf_op jit(solution)/shard_map/while/body/eval_jaxpr/cond/branch_1_fun/dot_general | solution.py:32
  528.1 24.0 %conditional.6 = (bf16[64,3072]{1,0:T(8,128)(2,1)S(1)}, bf16[64,3072]{1,0:T(8,128)(2,1)S(1)}, bf16[64,3072]{1,0:T(8,128)(2,1)}, f32[3072]{0:T(1024)}) conditional(s32[]{:T(128)} %convert_element_type.112, () %tuple.105, (bf16[4,64,3072]{2,1,0:T(8,128)(2,1)S(1)}, s32[]{:T(128)}, f32[1,3072]{1,0:T(1,128)S(1)}, pred[]{:T(512)}, ...), branch_computations={%region_6.6_spmd, %region_7.10_spmd} | conditional | flops 2424960000 | bytes 50776740 | solution.py:91
  528.5 10.3 %fusion.33 = bf16[64,3072]{1,0:T(8,128)(2,1)S(1)} fusion(bf16[64,3072]{1,0:T(8,128)(2,1)S(1)} %get-tuple-element.458, bf16[4,64,3072]{2,1,0:T(8,128)(2,1)} %get-tuple-element.457, s32[]{:T(128)} %get-tuple-element.454, pred[]{:T(512)} %get-tuple-element.456, bf16[64,3072]{1,0:T(8,128)(2,1)S(1)} %fusion.21, bf16[3072,3072]{1,0:T(8,128)(2,1)} %get-tuple-element.459), kind=kOutput, calls=%fused_computation.46 | convolution fusion | flops 1212284928 | bytes 20447236 | tf_op jit(solution)/shard_map/while/body/eval_jaxpr/cond/branch_1_fun/dot_general | solution.py:18
  538.8 10.5 %fusion.25 = (f32[3072]{0:T(1024)}, f32[64]{0:T(128)}, f32[64,3072]{1,0:T(8,128)S(1)}) fusion(f32[64]{0:T(128)S(1)} %add_rsqrt_fusion.1, bf16[4,64,3072]{2,1,0:T(8,128)(2,1)S(1)} %get-tuple-element.453, s32[]{:T(128)} %get-tuple-element.454, f32[3072]{0:T(1024)S(1)} %bitcast.60, bf16[64,3072]{1,0:T(8,128)(2,1)S(1)} %fusion.33, ...), kind=kOutput, calls=%fused_computation.38 | convolution fusion | flops 1209332736 | bytes 20472324 | tf_op jit(solution)/shard_map/while/body/eval_jaxpr/cond/branch_1_fun/dot_general | solution.py:32
  561.7 24.0 %conditional.6 = (bf16[64,3072]{1,0:T(8,128)(2,1)S(1)}, bf16[64,3072]{1,0:T(8,128)(2,1)S(1)}, bf16[64,3072]{1,0:T(8,128)(2,1)}, f32[3072]{0:T(1024)}) conditional(s32[]{:T(128)} %convert_element_type.112, () %tuple.105, (bf16[4,64,3072]{2,1,0:T(8,128)(2,1)S(1)}, s32[]{:T(128)}, f32[1,3072]{1,0:T(1,128)S(1)}, pred[]{:T(512)}, ...), branch_computations={%region_6.6_spmd, %region_7.10_spmd} | conditional | flops 2424960000 | bytes 50776740 | solution.py:91
  562.1 10.3 %fusion.33 = bf16[64,3072]{1,0:T(8,128)(2,1)S(1)} fusion(bf16[64,3072]{1,0:T(8,128)(2,1)S(1)} %get-tuple-element.458, bf16[4,64,3072]{2,1,0:T(8,128)(2,1)} %get-tuple-element.457, s32[]{:T(128)} %get-tuple-element.454, pred[]{:T(512)} %get-tuple-element.456, bf16[64,3072]{1,0:T(8,128)(2,1)S(1)} %fusion.21, bf16[3072,3072]{1,0:T(8,128)(2,1)} %get-tuple-element.459), kind=kOutput, calls=%fused_computation.46 | convolution fusion | flops 1212284928 | bytes 20447236 | tf_op jit(solution)/shard_map/while/body/eval_jaxpr/cond/branch_1_fun/dot_general | solution.py:18
  572.5 10.5 %fusion.25 = (f32[3072]{0:T(1024)}, f32[64]{0:T(128)}, f32[64,3072]{1,0:T(8,128)S(1)}) fusion(f32[64]{0:T(128)S(1)} %add_rsqrt_fusion.1, bf16[4,64,3072]{2,1,0:T(8,128)(2,1)S(1)} %get-tuple-element.453, s32[]{:T(128)} %get-tuple-element.454, f32[3072]{0:T(1024)S(1)} %bitcast.60, bf16[64,3072]{1,0:T(8,128)(2,1)S(1)} %fusion.33, ...), kind=kOutput, calls=%fused_computation.38 | convolution fusion | flops 1209332736 | bytes 20472324 | tf_op jit(solution)/shard_map/while/body/eval_jaxpr/cond/branch_1_fun/dot_general | solution.py:32
  594.5 11.0 %bitcast_convert_fusion = bf16[3072,3072]{1,0:T(8,128)(2,1)} fusion(bf16[4,64,3072]{2,1,0:T(8,128)(2,1)} %get-tuple-element.483, bf16[4,64,3072]{2,1,0:T(8,128)(2,1)} %get-tuple-element.484), kind=kOutput, calls=%fused_computation.61 | convolution fusion | flops 4841275392 | bytes 22020096 | tf_op jit(solution)/shard_map/dot_general | solution.py:119
  607.4 60.4 %all-reduce = bf16[3072]{0:T(1024)(128)(2,1)S(1)} all-reduce(bf16[3072]{0:T(1024)(128)(2,1)S(1)} %convert_element_type.68), channel_id=3, replica_groups=mesh['chain'=8,'dp'=16] {'dp'}, use_global_device_ids=true, to_apply=%region_13.14.clone | all-reduce | flops 3072 | bytes 12288
  668.5 121.6 %reduce-scatter.2.cloned.1.call-done = bf16[192,3072]{1,0:T(8,128)(2,1)} async-done(((bf16[3072,3072]{1,0:T(8,128)(2,1)}), bf16[192,3072]{1,0:T(8,128)(2,1)}) %reduce-scatter.2.cloned.1.call-update) | async-done | bytes 1179664 | tf_op jit(solution)/shard_map/reduce_scatter | solution.py:124
  (213 shorter events, 153.1 us)
Async XLA Ops:
  7.2 0.7 copy-start.4
  7.2 782.9 %reduce-scatter.2.cloned.1.call-start = ((), (), s32[]{:S(2)}) async-start(), calls=%async_computation.1 | async-start | bytes 20054016 | tf_op jit(solution)/shard_map/reduce_scatter | solution.py:124
  19.3 8.6 %collective-permute-start = (bf16[64,3072]{1,0:T(8,128)(2,1)S(1)}, bf16[64,3072]{1,0:T(8,128)(2,1)S(1)}, u32[]{:S(2)}, u32[]{:S(2)}) collective-permute-start(bf16[64,3072]{1,0:T(8,128)(2,1)S(1)} %get-tuple-element.792), channel_id=1, source_target_pairs={{0,16},{16,32},{32,48},{48,64},{64,80},{80,96},{96,112},{1,17},{17... | collective-permute-start | bytes 1179656 | tf_op jit(solution)/shard_map/while/body/eval_jaxpr/ppermute | solution.py:10
  39.3 10.4 %collective-permute-start = (bf16[64,3072]{1,0:T(8,128)(2,1)S(1)}, bf16[64,3072]{1,0:T(8,128)(2,1)S(1)}, u32[]{:S(2)}, u32[]{:S(2)}) collective-permute-start(bf16[64,3072]{1,0:T(8,128)(2,1)S(1)} %get-tuple-element.792), channel_id=1, source_target_pairs={{0,16},{16,32},{32,48},{48,64},{64,80},{80,96},{96,112},{1,17},{17... | collective-permute-start | bytes 1179656 | tf_op jit(solution)/shard_map/while/body/eval_jaxpr/ppermute | solution.py:10
  61.2 9.5 %collective-permute-start = (bf16[64,3072]{1,0:T(8,128)(2,1)S(1)}, bf16[64,3072]{1,0:T(8,128)(2,1)S(1)}, u32[]{:S(2)}, u32[]{:S(2)}) collective-permute-start(bf16[64,3072]{1,0:T(8,128)(2,1)S(1)} %get-tuple-element.792), channel_id=1, source_target_pairs={{0,16},{16,32},{32,48},{48,64},{64,80},{80,96},{96,112},{1,17},{17... | collective-permute-start | bytes 1179656 | tf_op jit(solution)/shard_map/while/body/eval_jaxpr/ppermute | solution.py:10
  82.1 8.8 %collective-permute-start = (bf16[64,3072]{1,0:T(8,128)(2,1)S(1)}, bf16[64,3072]{1,0:T(8,128)(2,1)S(1)}, u32[]{:S(2)}, u32[]{:S(2)}) collective-permute-start(bf16[64,3072]{1,0:T(8,128)(2,1)S(1)} %get-tuple-element.792), channel_id=1, source_target_pairs={{0,16},{16,32},{32,48},{48,64},{64,80},{80,96},{96,112},{1,17},{17... | collective-permute-start | bytes 1179656 | tf_op jit(solution)/shard_map/while/body/eval_jaxpr/ppermute | solution.py:10
  92.2 19.2 %collective-permute-start = (bf16[64,3072]{1,0:T(8,128)(2,1)S(1)}, bf16[64,3072]{1,0:T(8,128)(2,1)S(1)}, u32[]{:S(2)}, u32[]{:S(2)}) collective-permute-start(bf16[64,3072]{1,0:T(8,128)(2,1)S(1)} %get-tuple-element.792), channel_id=1, source_target_pairs={{0,16},{16,32},{32,48},{48,64},{64,80},{80,96},{96,112},{1,17},{17... | collective-permute-start | bytes 1179656 | tf_op jit(solution)/shard_map/while/body/eval_jaxpr/ppermute | solution.py:10
  112.6 9.8 %collective-permute-start = (bf16[64,3072]{1,0:T(8,128)(2,1)S(1)}, bf16[64,3072]{1,0:T(8,128)(2,1)S(1)}, u32[]{:S(2)}, u32[]{:S(2)}) collective-permute-start(bf16[64,3072]{1,0:T(8,128)(2,1)S(1)} %get-tuple-element.792), channel_id=1, source_target_pairs={{0,16},{16,32},{32,48},{48,64},{64,80},{80,96},{96,112},{1,17},{17... | collective-permute-start | bytes 1179656 | tf_op jit(solution)/shard_map/while/body/eval_jaxpr/ppermute | solution.py:10
  123.7 19.6 %collective-permute-start = (bf16[64,3072]{1,0:T(8,128)(2,1)S(1)}, bf16[64,3072]{1,0:T(8,128)(2,1)S(1)}, u32[]{:S(2)}, u32[]{:S(2)}) collective-permute-start(bf16[64,3072]{1,0:T(8,128)(2,1)S(1)} %get-tuple-element.792), channel_id=1, source_target_pairs={{0,16},{16,32},{32,48},{48,64},{64,80},{80,96},{96,112},{1,17},{17... | collective-permute-start | bytes 1179656 | tf_op jit(solution)/shard_map/while/body/eval_jaxpr/ppermute | solution.py:10
  144.5 10.0 %collective-permute-start = (bf16[64,3072]{1,0:T(8,128)(2,1)S(1)}, bf16[64,3072]{1,0:T(8,128)(2,1)S(1)}, u32[]{:S(2)}, u32[]{:S(2)}) collective-permute-start(bf16[64,3072]{1,0:T(8,128)(2,1)S(1)} %get-tuple-element.792), channel_id=1, source_target_pairs={{0,16},{16,32},{32,48},{48,64},{64,80},{80,96},{96,112},{1,17},{17... | collective-permute-start | bytes 1179656 | tf_op jit(solution)/shard_map/while/body/eval_jaxpr/ppermute | solution.py:10
  155.7 15.4 %collective-permute-start = (bf16[64,3072]{1,0:T(8,128)(2,1)S(1)}, bf16[64,3072]{1,0:T(8,128)(2,1)S(1)}, u32[]{:S(2)}, u32[]{:S(2)}) collective-permute-start(bf16[64,3072]{1,0:T(8,128)(2,1)S(1)} %get-tuple-element.792), channel_id=1, source_target_pairs={{0,16},{16,32},{32,48},{48,64},{64,80},{80,96},{96,112},{1,17},{17... | collective-permute-start | bytes 1179656 | tf_op jit(solution)/shard_map/while/body/eval_jaxpr/ppermute | solution.py:10
  172.4 15.2 %collective-permute-start = (bf16[64,3072]{1,0:T(8,128)(2,1)S(1)}, bf16[64,3072]{1,0:T(8,128)(2,1)S(1)}, u32[]{:S(2)}, u32[]{:S(2)}) collective-permute-start(bf16[64,3072]{1,0:T(8,128)(2,1)S(1)} %get-tuple-element.792), channel_id=1, source_target_pairs={{0,16},{16,32},{32,48},{48,64},{64,80},{80,96},{96,112},{1,17},{17... | collective-permute-start | bytes 1179656 | tf_op jit(solution)/shard_map/while/body/eval_jaxpr/ppermute | solution.py:10
  188.9 12.7 %collective-permute-start = (bf16[64,3072]{1,0:T(8,128)(2,1)S(1)}, bf16[64,3072]{1,0:T(8,128)(2,1)S(1)}, u32[]{:S(2)}, u32[]{:S(2)}) collective-permute-start(bf16[64,3072]{1,0:T(8,128)(2,1)S(1)} %get-tuple-element.792), channel_id=1, source_target_pairs={{0,16},{16,32},{32,48},{48,64},{64,80},{80,96},{96,112},{1,17},{17... | collective-permute-start | bytes 1179656 | tf_op jit(solution)/shard_map/while/body/eval_jaxpr/ppermute | solution.py:10
  205.7 15.9 %collective-permute-start.1 = (bf16[64,3072]{1,0:T(8,128)(2,1)}, bf16[64,3072]{1,0:T(8,128)(2,1)S(1)}, u32[]{:S(2)}, u32[]{:S(2)}) collective-permute-start(bf16[64,3072]{1,0:T(8,128)(2,1)} %get-tuple-element.697), channel_id=1, source_target_pairs={{16,0},{32,16},{48,32},{64,48},{80,64},{96,80},{112,96},{17,1},{33... | collective-permute-start | bytes 1179656 | tf_op jit(solution)/shard_map/while/body/eval_jaxpr/ppermute | solution.py:10
  223.0 14.0 %collective-permute-start.1 = (bf16[64,3072]{1,0:T(8,128)(2,1)}, bf16[64,3072]{1,0:T(8,128)(2,1)S(1)}, u32[]{:S(2)}, u32[]{:S(2)}) collective-permute-start(bf16[64,3072]{1,0:T(8,128)(2,1)} %get-tuple-element.697), channel_id=1, source_target_pairs={{16,0},{32,16},{48,32},{64,48},{80,64},{96,80},{112,96},{17,1},{33... | collective-permute-start | bytes 1179656 | tf_op jit(solution)/shard_map/while/body/eval_jaxpr/ppermute | solution.py:10
  238.4 20.4 %collective-permute-start.1 = (bf16[64,3072]{1,0:T(8,128)(2,1)}, bf16[64,3072]{1,0:T(8,128)(2,1)S(1)}, u32[]{:S(2)}, u32[]{:S(2)}) collective-permute-start(bf16[64,3072]{1,0:T(8,128)(2,1)} %get-tuple-element.697), channel_id=1, source_target_pairs={{16,0},{32,16},{48,32},{64,48},{80,64},{96,80},{112,96},{17,1},{33... | collective-permute-start | bytes 1179656 | tf_op jit(solution)/shard_map/while/body/eval_jaxpr/ppermute | solution.py:10
  260.2 14.4 %collective-permute-start.1 = (bf16[64,3072]{1,0:T(8,128)(2,1)}, bf16[64,3072]{1,0:T(8,128)(2,1)S(1)}, u32[]{:S(2)}, u32[]{:S(2)}) collective-permute-start(bf16[64,3072]{1,0:T(8,128)(2,1)} %get-tuple-element.697), channel_id=1, source_target_pairs={{16,0},{32,16},{48,32},{64,48},{80,64},{96,80},{112,96},{17,1},{33... | collective-permute-start | bytes 1179656 | tf_op jit(solution)/shard_map/while/body/eval_jaxpr/ppermute | solution.py:10
  276.1 16.1 %collective-permute-start.1 = (bf16[64,3072]{1,0:T(8,128)(2,1)}, bf16[64,3072]{1,0:T(8,128)(2,1)S(1)}, u32[]{:S(2)}, u32[]{:S(2)}) collective-permute-start(bf16[64,3072]{1,0:T(8,128)(2,1)} %get-tuple-element.697), channel_id=1, source_target_pairs={{16,0},{32,16},{48,32},{64,48},{80,64},{96,80},{112,96},{17,1},{33... | collective-permute-start | bytes 1179656 | tf_op jit(solution)/shard_map/while/body/eval_jaxpr/ppermute | solution.py:10
  293.6 14.4 %collective-permute-start.1 = (bf16[64,3072]{1,0:T(8,128)(2,1)}, bf16[64,3072]{1,0:T(8,128)(2,1)S(1)}, u32[]{:S(2)}, u32[]{:S(2)}) collective-permute-start(bf16[64,3072]{1,0:T(8,128)(2,1)} %get-tuple-element.697), channel_id=1, source_target_pairs={{16,0},{32,16},{48,32},{64,48},{80,64},{96,80},{112,96},{17,1},{33... | collective-permute-start | bytes 1179656 | tf_op jit(solution)/shard_map/while/body/eval_jaxpr/ppermute | solution.py:10
  309.4 151.3 %collective-permute-start.1 = (bf16[64,3072]{1,0:T(8,128)(2,1)}, bf16[64,3072]{1,0:T(8,128)(2,1)S(1)}, u32[]{:S(2)}, u32[]{:S(2)}) collective-permute-start(bf16[64,3072]{1,0:T(8,128)(2,1)} %get-tuple-element.697), channel_id=1, source_target_pairs={{16,0},{32,16},{48,32},{64,48},{80,64},{96,80},{112,96},{17,1},{33... | collective-permute-start | bytes 1179656 | tf_op jit(solution)/shard_map/while/body/eval_jaxpr/ppermute | solution.py:10
  461.2 10.4 %copy-start = (bf16[64,3072]{1,0:T(8,128)(2,1)}, bf16[64,3072]{1,0:T(8,128)(2,1)S(1)}, u32[]{:S(2)}) copy-start(bf16[64,3072]{1,0:T(8,128)(2,1)S(1)} %fusion.21) | copy-start | bytes 1179652 | tf_op jit(solution)/shard_map/while/body/eval_jaxpr/cond
  471.5 10.5 %copy-start.2 = (bf16[64,3072]{1,0:T(8,128)(2,1)}, bf16[64,3072]{1,0:T(8,128)(2,1)S(1)}, u32[]{:S(2)}) copy-start(bf16[64,3072]{1,0:T(8,128)(2,1)S(1)} %fusion.33) | copy-start | bytes 1179652 | tf_op jit(solution)/shard_map/while/body/eval_jaxpr/cond
  482.0 2.8 copy-start.1
  482.0 2.8 copy-start.3
  484.8 9.6 %collective-permute-start.1 = (bf16[64,3072]{1,0:T(8,128)(2,1)}, bf16[64,3072]{1,0:T(8,128)(2,1)S(1)}, u32[]{:S(2)}, u32[]{:S(2)}) collective-permute-start(bf16[64,3072]{1,0:T(8,128)(2,1)} %get-tuple-element.697), channel_id=1, source_target_pairs={{16,0},{32,16},{48,32},{64,48},{80,64},{96,80},{112,96},{17,1},{33... | collective-permute-start | bytes 1179656 | tf_op jit(solution)/shard_map/while/body/eval_jaxpr/ppermute | solution.py:10
  494.8 10.4 %copy-start = (bf16[64,3072]{1,0:T(8,128)(2,1)}, bf16[64,3072]{1,0:T(8,128)(2,1)S(1)}, u32[]{:S(2)}) copy-start(bf16[64,3072]{1,0:T(8,128)(2,1)S(1)} %fusion.21) | copy-start | bytes 1179652 | tf_op jit(solution)/shard_map/while/body/eval_jaxpr/cond
  505.2 10.5 %copy-start.2 = (bf16[64,3072]{1,0:T(8,128)(2,1)}, bf16[64,3072]{1,0:T(8,128)(2,1)S(1)}, u32[]{:S(2)}) copy-start(bf16[64,3072]{1,0:T(8,128)(2,1)S(1)} %fusion.33) | copy-start | bytes 1179652 | tf_op jit(solution)/shard_map/while/body/eval_jaxpr/cond
  515.7 2.8 copy-start.1
  515.7 2.8 copy-start.3
  518.5 9.6 %collective-permute-start.1 = (bf16[64,3072]{1,0:T(8,128)(2,1)}, bf16[64,3072]{1,0:T(8,128)(2,1)S(1)}, u32[]{:S(2)}, u32[]{:S(2)}) collective-permute-start(bf16[64,3072]{1,0:T(8,128)(2,1)} %get-tuple-element.697), channel_id=1, source_target_pairs={{16,0},{32,16},{48,32},{64,48},{80,64},{96,80},{112,96},{17,1},{33... | collective-permute-start | bytes 1179656 | tf_op jit(solution)/shard_map/while/body/eval_jaxpr/ppermute | solution.py:10
  528.4 10.4 %copy-start = (bf16[64,3072]{1,0:T(8,128)(2,1)}, bf16[64,3072]{1,0:T(8,128)(2,1)S(1)}, u32[]{:S(2)}) copy-start(bf16[64,3072]{1,0:T(8,128)(2,1)S(1)} %fusion.21) | copy-start | bytes 1179652 | tf_op jit(solution)/shard_map/while/body/eval_jaxpr/cond
  538.8 10.5 %copy-start.2 = (bf16[64,3072]{1,0:T(8,128)(2,1)}, bf16[64,3072]{1,0:T(8,128)(2,1)S(1)}, u32[]{:S(2)}) copy-start(bf16[64,3072]{1,0:T(8,128)(2,1)S(1)} %fusion.33) | copy-start | bytes 1179652 | tf_op jit(solution)/shard_map/while/body/eval_jaxpr/cond
  549.3 2.8 copy-start.1
  549.3 2.8 copy-start.3
  552.1 9.6 %collective-permute-start.1 = (bf16[64,3072]{1,0:T(8,128)(2,1)}, bf16[64,3072]{1,0:T(8,128)(2,1)S(1)}, u32[]{:S(2)}, u32[]{:S(2)}) collective-permute-start(bf16[64,3072]{1,0:T(8,128)(2,1)} %get-tuple-element.697), channel_id=1, source_target_pairs={{16,0},{32,16},{48,32},{64,48},{80,64},{96,80},{112,96},{17,1},{33... | collective-permute-start | bytes 1179656 | tf_op jit(solution)/shard_map/while/body/eval_jaxpr/ppermute | solution.py:10
  562.1 10.4 %copy-start = (bf16[64,3072]{1,0:T(8,128)(2,1)}, bf16[64,3072]{1,0:T(8,128)(2,1)S(1)}, u32[]{:S(2)}) copy-start(bf16[64,3072]{1,0:T(8,128)(2,1)S(1)} %fusion.21) | copy-start | bytes 1179652 | tf_op jit(solution)/shard_map/while/body/eval_jaxpr/cond
  572.5 10.5 %copy-start.2 = (bf16[64,3072]{1,0:T(8,128)(2,1)}, bf16[64,3072]{1,0:T(8,128)(2,1)S(1)}, u32[]{:S(2)}) copy-start(bf16[64,3072]{1,0:T(8,128)(2,1)S(1)} %fusion.33) | copy-start | bytes 1179652 | tf_op jit(solution)/shard_map/while/body/eval_jaxpr/cond
  583.0 2.8 copy-start.1
  583.0 2.8 copy-start.3
  585.7 8.7 %collective-permute-start.1 = (bf16[64,3072]{1,0:T(8,128)(2,1)}, bf16[64,3072]{1,0:T(8,128)(2,1)S(1)}, u32[]{:S(2)}, u32[]{:S(2)}) collective-permute-start(bf16[64,3072]{1,0:T(8,128)(2,1)} %get-tuple-element.697), channel_id=1, source_target_pairs={{16,0},{32,16},{48,32},{64,48},{80,64},{96,80},{112,96},{17,1},{33... | collective-permute-start | bytes 1179656 | tf_op jit(solution)/shard_map/while/body/eval_jaxpr/ppermute | solution.py:10
  605.4 0.7 copy-start.5
  605.4 0.7 copy-start.6
Sparse Core Ops, SparseCore 0:
  605.6 184.4 reduce-scatter.1
where the time goes:
time: 800 us; the launch traced here: 797 us
  waiting for transfers between devices  403 us (50%)
  matrix products  134 us (17%)
  starting transfers between devices  92.4 us (12%)
  blocking collectives  60.4 us (8%)
  other arithmetic  53.2 us (7%)
  local copies, waits for them, and re-layouts  37.7 us (5%)
  between operations  14.7 us (2%)
    ppermute x22, waiting for transfers between devices, passed_along(): return lax.ppermute(block, axis, route)  281 us
    reduce_scatter x1, waiting for transfers between devices, on_device(): lax.psum_scatter(weight_part.astype(jnp.bfloat16), 'dp', scatter_dimensio...  122 us
    ppermute x22, starting transfers between devices, passed_along(): return lax.ppermute(block, axis, route)  92.4 us
    dot_general x8, matrix products, layer_parts(): hidden = jnp.dot(scaled, weight, preferred_element_type=jnp.float32)  81.4 us
    unnamed x1, blocking collectives  60.4 us
    dot_general x4, matrix products, retreat(): lax.dot_general(grad_hidden, weight, (((1,), (1,)), ((), ())), preferred_...  42 us
  transfers between devices with their start and end apart: 23, of which 23 were waited for; matrix products, arithmetic and copies ran while one was open for 6% of the time, Pallas kernels for 0%

commit v1 on v0

v1 whole, which is shorter than its diff:
```python
import functools

import jax
import jax.numpy as jnp
from jax import lax
from jax.experimental import pallas as pl
from jax.experimental.pallas import tpu as pltpu
from jax.sharding import PartitionSpec as P

SECTIONS = 8
MB = 4
LAST = SECTIONS - 1
TURN = 2 * LAST
VM = pl.BlockSpec(memory_space=pltpu.VMEM)
SM = pl.BlockSpec(memory_space=pltpu.SMEM)
COLS = 1024
PIECES = 6


def pin(array):
    return pltpu.with_memory_space_constraint(array, pltpu.VMEM)


def params(mib):
    return pltpu.CompilerParams(vmem_limit_bytes=mib << 20)


def partner(section, replica):
    z_hi, rest = divmod(replica, 8)
    core = rest % 2
    if section % 2 == 0 and core == 1:
        z_hi = 1 - z_hi
    return z_hi * 8 + rest


def route(sections, forward, replicas):
    pairs = []
    for section in sections:
        low = section if forward else section - 1
        for replica in range(replicas):
            here, there = low * replicas + replica, (low + 1) * replicas + partner(low, replica)
            pairs.append((here, there) if forward else (there, here))
    return pairs


def load_kernel(weight_hbm, weight_ref, turned_ref, hidden_ref, input_ref, scaled_ref, grad_ref, sem):
    copy = pltpu.make_async_copy(weight_hbm, weight_ref, sem)
    copy.start()
    copy.wait()


def load(weight, micro, rows, channels):
    kept = (micro, rows, channels)
    return pl.pallas_call(
        load_kernel,
        out_shape=[
            pltpu.VMEM((channels, channels), jnp.bfloat16),
            pltpu.VMEM((channels, channels), jnp.bfloat16),
            pltpu.VMEM(kept, jnp.float32),
            pltpu.VMEM(kept, jnp.bfloat16),
            pltpu.VMEM(kept, jnp.bfloat16),
            pltpu.VMEM(kept, jnp.bfloat16),
        ],
        in_specs=[pl.BlockSpec(memory_space=pl.ANY)],
        out_specs=[VM] * 6,
        scratch_shapes=[pltpu.SemaphoreType.DMA],
        name="load_weight",
        compiler_params=params(4),
    )(weight)


def turn_kernel(piece, weight_ref, turned_in, after_ref, turned_ref, token_ref):
    rows = weight_ref.shape[0] // PIECES
    step = 256
    for start in range(piece * rows, (piece + 1) * rows, step):
        turned_ref[:, start : start + step] = weight_ref[start : start + step, :].T
    token_ref[0] = 0


def turn(piece, weight, turned, after):
    return pl.pallas_call(
        functools.partial(turn_kernel, piece),
        out_shape=[
            jax.ShapeDtypeStruct(turned.shape, turned.dtype),
            jax.ShapeDtypeStruct((1,), jnp.int32),
        ],
        in_specs=[VM, VM, VM],
        out_specs=[VM, SM],
        input_output_aliases={1: 0},
        name="turn_weight",
        compiler_params=params(4),
    )(pin(weight), pin(turned), pin(after))


def forward_kernel(
    moment, section_ref, token_ref, given_ref, first_ref, gain_ref, weight_ref, _h, _i, _s,
    output_ref, hidden_ref, input_ref, scaled_ref,
):
    section = section_ref[0]
    slot = moment - section
    micro = hidden_ref.shape[0]

    @pl.when(jnp.logical_and(slot >= 0, slot < micro))
    def _():
        given = given_ref[...]
        if moment < micro:
            given = jnp.where(section == 0, first_ref[moment], given)
        input_ref[slot] = given
        x_float = given.astype(jnp.float32)
        inv_rms = lax.rsqrt(jnp.mean(x_float * x_float, axis=-1, keepdims=True) + 1e-06)
        scaled_ref[slot] = (x_float * inv_rms * gain_ref[...]).astype(jnp.bfloat16)
        for start in range(0, x_float.shape[1], COLS):
            part = slice(start, start + COLS)
            hidden = jnp.dot(scaled_ref[slot], weight_ref[:, part], preferred_element_type=jnp.float32)
            hidden_ref[slot, :, part] = hidden
            x_part = input_ref[slot, :, part].astype(jnp.float32)
            output_ref[:, part] = (x_part + jax.nn.gelu(hidden)).astype(jnp.bfloat16)


def forward(moment, section, token, given, first, gain, weight, kept):
    rows = jax.ShapeDtypeStruct(given.shape, given.dtype)
    hidden, inputs, scaled = kept
    return pl.pallas_call(
        functools.partial(forward_kernel, moment),
        out_shape=[pltpu.VMEM(rows.shape, rows.dtype)]
        + [jax.ShapeDtypeStruct(a.shape, a.dtype) for a in kept],
        in_specs=[SM, SM, VM, VM, VM, VM, VM, VM, VM],
        out_specs=[VM] * 4,
        input_output_aliases={6: 1, 7: 2, 8: 3},
        name=f"forward_step_{moment}",
        compiler_params=params(8),
    )(section, token, pin(given), pin(first), pin(gain), pin(weight), pin(hidden), pin(inputs), pin(scaled))


def backward_kernel(
    moment, section_ref, given_ref, last_ref, gain_ref, turned_ref, hidden_ref, input_ref, _g,
    output_ref, grad_ref, sum_ref,
):
    section = section_ref[0]
    slot = moment - TURN + section
    micro, rows, channels = hidden_ref.shape

    def upstream(part):
        given = given_ref[:, part]
        if 0 <= moment - LAST < micro:
            given = jnp.where(section == LAST, last_ref[moment - LAST, :, part], given)
        return given.astype(jnp.float32)

    active = jnp.logical_and(slot >= 0, slot < micro)

    @pl.when(active)
    def _():
        for start in range(0, channels, COLS):
            part = slice(start, start + COLS)
            _, pullback = jax.vjp(jax.nn.gelu, hidden_ref[slot, :, part])
            grad_ref[slot, :, part] = pullback(upstream(part))[0].astype(jnp.bfloat16)

    @pl.when(jnp.logical_and(active, section > 0))
    def _():
        x_float = input_ref[slot].astype(jnp.float32)
        inv_rms = lax.rsqrt(jnp.mean(x_float * x_float, axis=-1, keepdims=True) + 1e-06)
        total = jnp.zeros((rows, 1), jnp.float32)
        for start in range(0, channels, COLS):
            part = slice(start, start + COLS)
            grad_normed = gain_ref[:, part] * jnp.dot(
                grad_ref[slot], turned_ref[:, part], preferred_element_type=jnp.float32
            )
            sum_ref[:, part] = grad_normed
            normed = input_ref[slot, :, part].astype(jnp.float32) * inv_rms
            total = total + jnp.sum(grad_normed * normed, axis=-1, keepdims=True)
        mean = total * (1.0 / channels)
        for start in range(0, channels, COLS):
            part = slice(start, start + COLS)
            normed = input_ref[slot, :, part].astype(jnp.float32) * inv_rms
            grad_input = upstream(part) + inv_rms * (sum_ref[:, part] - normed * mean)
            output_ref[:, part] = grad_input.astype(jnp.bfloat16)


def backward(moment, section, given, last, gain, turned, hidden, inputs, grads):
    return pl.pallas_call(
        functools.partial(backward_kernel, moment),
        out_shape=[
            pltpu.VMEM(given.shape, given.dtype),
            jax.ShapeDtypeStruct(grads.shape, grads.dtype),
        ],
        in_specs=[SM, VM, VM, VM, VM, VM, VM, VM],
        out_specs=[VM] * 2,
        input_output_aliases={7: 1},
        scratch_shapes=[pltpu.VMEM(given.shape, jnp.float32)],
        name=f"backward_step_{moment}",
        compiler_params=params(8),
    )(section, pin(given), pin(last), pin(gain), pin(turned), pin(hidden), pin(inputs), pin(grads))


def on_device(tokens, cotangent, weights, gains):
    replicas = lax.axis_size("dp")
    micro, rows, channels = tokens.shape
    section = lax.axis_index("chain").astype(jnp.int32).reshape(1)
    gain = gains
    axes = ("chain", "dp")

    weight, turned, hidden, inputs, scaled, grads = load(weights[0], micro, rows, channels)
    token = jnp.zeros((1,), jnp.int32)
    arriving = tokens[0]
    returning = cotangent[0]
    for moment in range(TURN + micro):
        sent = None
        if moment < LAST + micro:
            output, hidden, inputs, scaled = forward(
                moment, section, token, arriving, tokens, gain, weight, (hidden, inputs, scaled)
            )
            senders = [s for s in range(LAST) if 0 <= moment - s < micro]
            if senders:
                sent = lax.ppermute(output, axes, route(senders, True, replicas))
            if moment < PIECES:
                turned, token = turn(moment, weight, turned, output)
        if moment >= LAST:
            output, grads = backward(
                moment, section, returning, cotangent, gain, turned, hidden, inputs, grads
            )
            senders = [s for s in range(1, SECTIONS) if 0 <= moment - TURN + s < micro]
            if senders:
                returning = lax.ppermute(output, axes, route(senders, False, replicas))
        if sent is not None:
            arriving = sent

    span = micro * rows
    every_scaled = lax.all_gather(scaled.reshape(span, channels), "dp", axis=0, tiled=True)
    share = channels // replicas
    columns = grads.reshape(span, replicas, share).transpose(1, 0, 2)
    columns = lax.all_to_all(columns, "dp", 0, 0).reshape(replicas * span, share)
    product = lax.dot_general(
        every_scaled, columns, (((0,), (0,)), ((), ())), preferred_element_type=jnp.float32
    ).astype(jnp.bfloat16)
    blocks = lax.all_to_all(product.reshape(replicas, share, share), "dp", 0, 0)
    weight_rows = blocks.transpose(1, 0, 2).reshape(share, channels)
    start = lax.axis_index("dp") * share
    own = lax.dynamic_slice_in_dim(weights[0], start, share, 0).astype(jnp.float32)
    own_gain = lax.dynamic_slice_in_dim(gains[0], start, share, 0)
    gain_rows = jnp.sum(own * weight_rows.astype(jnp.float32), axis=-1) / own_gain
    return (weight_rows[None], gain_rows[None])


def solution(mesh):
    placed = (P(None, "dp", None), P(None, "dp", None), P("chain", None, None), P("chain", None))
    return jax.shard_map(
        on_device,
        mesh=mesh,
        in_specs=placed,
        out_specs=(P("chain", "dp", None), P("chain", "dp")),
        check_vma=False,
    )
```

time: 800 us -> 489 us (0.61)
  waiting for transfers between devices: 403 us -> 252 us
  matrix products: 134 us -> 11 us
  starting transfers between devices: 92.4 us -> 40.2 us
  other arithmetic: 53.2 us -> 4.91 us
  Pallas kernels: 0 us -> 43.4 us
  local copies, waits for them, and re-layouts: 37.7 us -> 73.2 us
  blocking collectives: 60.4 us -> 40 us
    dot_general x13 -> x1, matrix products: 134 us -> 11 us  [on_device(): lax.dot_general(every_scaled, columns, (((0,), (0,)), ((), ())), preferre...]
    reduce_scatter x1 -> x0, waiting for transfers between devices: 122 us -> none  [on_device(): lax.psum_scatter(weight_part.astype(jnp.bfloat16), 'dp', scatter_dimensio...]
    unnamed x1 -> x0, blocking collectives: 60.4 us -> none
    unnamed x7 -> x41, local copies, waits for them, and re-layouts: 1.68 us -> 59.5 us
    ppermute x22 -> x20, starting transfers between devices: 92.4 us -> 35.6 us  [the longest x10 26.4 us: on_device(): sent = lax.ppermute(output, axes, route(senders, True, replicas))]
    ppermute x22 -> x20, waiting for transfers between devices: 281 us -> 229 us  [the longest x10 218 us: on_device(): returning = lax.ppermute(output, axes, route(senders, False, replicas))]
    pallas_call x0 -> x29, Pallas kernels: none -> 43.4 us  [the longest x11 22.9 us: forward(): pl.pallas_call(functools.partial(forward_kernel, moment), out_shape=[pltp...]
    all_to_all x0 -> x1, blocking collectives: none -> 40 us  [on_device(): lax.all_to_all(columns, 'dp', 0, 0).reshape(replicas * span, share)]
  transfers between devices with their start and end apart: 23 -> 22, of which waited for: 23 -> 8; matrix products, arithmetic and copies ran while one was open for 6% -> 1% of each run, Pallas kernels for 0% -> 3%
where the time goes in v1:
time: 489 us; the launch traced here: 480 us
  waiting for transfers between devices  252 us (52%)
  local copies, waits for them, and re-layouts  73.2 us (15%)
  Pallas kernels  43.4 us (9%)
  starting transfers between devices  40.2 us (8%)
  blocking collectives  40 us (8%)
  between operations  15.1 us (3%)
  matrix products  11 us (2%)
  other arithmetic  4.91 us (1%)
    ppermute x10, waiting for transfers between devices, on_device(): returning = lax.ppermute(output, axes, route(senders, False, replicas))  218 us
    unnamed x41, local copies, waits for them, and re-layouts  59.5 us
    all_to_all x1, blocking collectives, on_device(): lax.all_to_all(columns, 'dp', 0, 0).reshape(replicas * span, share)  40 us
    ppermute x10, starting transfers between devices, on_device(): sent = lax.ppermute(output, axes, route(senders, True, replicas))  26.4 us
    all_to_all x1, waiting for transfers between devices, on_device(): blocks = lax.all_to_all(product.reshape(replicas, share, share), 'dp', 0, 0)  23.1 us
    pallas_call x11, Pallas kernels, forward(): pl.pallas_call(functools.partial(forward_kernel, moment), out_shape=[pltp...  22.9 us
    ppermute x10, waiting for transfers between devices, on_device(): sent = lax.ppermute(output, axes, route(senders, True, replicas))  11.2 us
    dot_general x1, matrix products, on_device(): lax.dot_general(every_scaled, columns, (((0,), (0,)), ((), ())), preferre...  11 us
  transfers between devices with their start and end apart: 22, of which 8 were waited for; matrix products, arithmetic and copies ran while one was open for 1% of the time, Pallas kernels for 3%

profile of v1, /device:TPU:1, one launch (start us, length us, event | category | flops | bytes accessed | tf_op | source)
XLA Modules:
  0.0 479.9 jit_solution(15481521706606501514)
XLA Ops:
  7.2 6.5 %load_weight.1 = (bf16[3072,3072]{1,0:T(8,128)(2,1)S(1)}, bf16[3072,3072]{1,0:T(8,128)(2,1)S(1)}, f32[4,64,3072]{2,1,0:T(8,128)S(1)}, bf16[4,64,3072]{2,1,0:T(8,...) custom-call(bf16[3072,3072]{1,0:T(8,128)(2,1)} %bitcast.26), custom_call_target="tpu_custom_call" | custom-call | tf_op jit(solution)/shard_map/load_weight/pallas_call | solution.py:54
  13.7 6.4 %copy-done = bf16[3072,3072]{1,0:T(8,128)(2,1)} copy-done((bf16[3072,3072]{1,0:T(8,128)(2,1)}, bf16[3072,3072]{1,0:T(8,128)(2,1)S(1)}, u32[]{:S(2)}) %copy-start) | copy-done | bytes 18874392
  20.2 6.5 %copy-done.3 = bf16[3072,3072]{1,0:T(8,128)(2,1)} copy-done((bf16[3072,3072]{1,0:T(8,128)(2,1)}, bf16[3072,3072]{1,0:T(8,128)(2,1)S(1)}, u32[]{:S(2)}) %copy-start.3) | copy-done | bytes 18874392
  26.7 6.4 %copy-done.1 = bf16[3072,3072]{1,0:T(8,128)(2,1)S(1)} copy-done((bf16[3072,3072]{1,0:T(8,128)(2,1)S(1)}, bf16[3072,3072]{1,0:T(8,128)(2,1)}, u32[]{:S(2)}) %copy-start.1) | copy-done | bytes 18874392
  33.0 3.6 forward_step_0.1
  36.7 3.1 collective-permute-start
  39.8 6.4 %copy-done.4 = bf16[3072,3072]{1,0:T(8,128)(2,1)S(1)} copy-done((bf16[3072,3072]{1,0:T(8,128)(2,1)S(1)}, bf16[3072,3072]{1,0:T(8,128)(2,1)}, u32[]{:S(2)}) %copy-start.4) | copy-done | bytes 18874392
  47.2 6.4 %copy-done.5 = bf16[3072,3072]{1,0:T(8,128)(2,1)} copy-done((bf16[3072,3072]{1,0:T(8,128)(2,1)}, bf16[3072,3072]{1,0:T(8,128)(2,1)S(1)}, u32[]{:S(2)}) %copy-start.5) | copy-done | bytes 18874392
  53.6 4.5 forward_step_1.1
  58.1 6.4 %collective-permute-start.1 = (bf16[64,3072]{1,0:T(8,128)(2,1)S(1)}, bf16[64,3072]{1,0:T(8,128)(2,1)S(1)}, u32[]{:S(2)}, u32[]{:S(2)}) collective-permute-start(bf16[64,3072]{1,0:T(8,128)(2,1)S(1)} %get-tuple-element.95.after_ref), channel_id=1, source_target_pairs={{0,16},{1,25},{2,18},{3,27},{4,20},{5,29},{6,22},{7,31},{8,24},{9,... | collective-permute-start | bytes 1179656 | tf_op jit(solution)/shard_map/ppermute | solution.py:214
  65.4 3.7 collective-permute-done.1.given_ref
  69.1 4.3 forward_step_2.1
  73.4 5.3 %collective-permute-start.2 = (bf16[64,3072]{1,0:T(8,128)(2,1)S(1)}, bf16[64,3072]{1,0:T(8,128)(2,1)S(1)}, u32[]{:S(2)}, u32[]{:S(2)}) collective-permute-start(bf16[64,3072]{1,0:T(8,128)(2,1)S(1)} %get-tuple-element.101.after_ref), channel_id=1, source_target_pairs={{0,16},{1,25},{2,18},{3,27},{4,20},{5,29},{6,22},{7,31},{8,24},{9,... | collective-permute-start | bytes 1179656 | tf_op jit(solution)/shard_map/ppermute | solution.py:214
  79.7 3.7 collective-permute-done.2.given_ref
  83.4 4.8 forward_step_3.1
  88.2 7.5 %collective-permute-start.3 = (bf16[64,3072]{1,0:T(8,128)(2,1)S(1)}, bf16[64,3072]{1,0:T(8,128)(2,1)S(1)}, u32[]{:S(2)}, u32[]{:S(2)}) collective-permute-start(bf16[64,3072]{1,0:T(8,128)(2,1)S(1)} %get-tuple-element.107.after_ref), channel_id=1, source_target_pairs={{0,16},{1,25},{2,18},{3,27},{4,20},{5,29},{6,22},{7,31},{8,24},{9,... | collective-permute-start | bytes 1179656 | tf_op jit(solution)/shard_map/ppermute | solution.py:214
  96.6 3.7 collective-permute-done.3.given_ref
  105.8 5.5 %copy-done.7 = bf16[3072,3072]{1,0:T(8,128)(2,1)} copy-done((bf16[3072,3072]{1,0:T(8,128)(2,1)}, bf16[3072,3072]{1,0:T(8,128)(2,1)S(1)}, u32[]{:S(2)}) %copy-start.7) | copy-done | bytes 18874392
  113.6 6.4 %copy-done.8 = bf16[3072,3072]{1,0:T(8,128)(2,1)S(1)} copy-done((bf16[3072,3072]{1,0:T(8,128)(2,1)S(1)}, bf16[3072,3072]{1,0:T(8,128)(2,1)}, u32[]{:S(2)}) %copy-start.8) | copy-done | bytes 18874392
  124.3 4.5 backward_step_9.1
  128.9 1.4 forward_step_10.1
  131.4 1.1 copy-done.15
  133.3 6.4 %copy-done.9 = bf16[3072,3072]{1,0:T(8,128)(2,1)S(1)} copy-done((bf16[3072,3072]{1,0:T(8,128)(2,1)S(1)}, bf16[3072,3072]{1,0:T(8,128)(2,1)}, u32[]{:S(2)}) %copy-start.9) | copy-done | bytes 18874392
  139.7 1.4 copy-done.11
  141.1 1.4 copy-done.13
  142.5 1.4 copy-done.17
  146.2 1.3 collective-permute-start.16
  147.5 129.4 %collective-permute-done.16.given_ref = bf16[64,3072]{1,0:T(8,128)(2,1)S(1)} collective-permute-done((bf16[64,3072]{1,0:T(8,128)(2,1)S(1)}, bf16[64,3072]{1,0:T(8,128)(2,1)S(1)}, u32[]{:S(2)}, u32[]{:S(2)}) %collective-permute-start.16) | collective-permute-done | bytes 393248 | tf_op jit(solution)/shard_map/ppermute | solution.py:223
  277.7 1.3 collective-permute-start.17
  279.0 12.8 %collective-permute-done.17.given_ref = bf16[64,3072]{1,0:T(8,128)(2,1)S(1)} collective-permute-done((bf16[64,3072]{1,0:T(8,128)(2,1)S(1)}, bf16[64,3072]{1,0:T(8,128)(2,1)S(1)}, u32[]{:S(2)}, u32[]{:S(2)}) %collective-permute-start.17) | collective-permute-done | bytes 393248 | tf_op jit(solution)/shard_map/ppermute | solution.py:223
  292.3 1.3 collective-permute-start.18
  293.6 14.3 %collective-permute-done.18.given_ref = bf16[64,3072]{1,0:T(8,128)(2,1)S(1)} collective-permute-done((bf16[64,3072]{1,0:T(8,128)(2,1)S(1)}, bf16[64,3072]{1,0:T(8,128)(2,1)S(1)}, u32[]{:S(2)}, u32[]{:S(2)}) %collective-permute-start.18) | collective-permute-done | bytes 393248 | tf_op jit(solution)/shard_map/ppermute | solution.py:223
  308.5 1.3 collective-permute-start.19
  309.8 61.4 %collective-permute-done.19.given_ref = bf16[64,3072]{1,0:T(8,128)(2,1)S(1)} collective-permute-done((bf16[64,3072]{1,0:T(8,128)(2,1)S(1)}, bf16[64,3072]{1,0:T(8,128)(2,1)S(1)}, u32[]{:S(2)}, u32[]{:S(2)}) %collective-permute-start.19) | collective-permute-done | bytes 393248 | tf_op jit(solution)/shard_map/ppermute | solution.py:223
  371.1 1.6 backward_step_17.1
  372.7 1.2 copy-done.14
  373.9 3.7 reshape.29
  377.6 2.9 copy.61
  380.5 40.0 %all_to_all.10 = bf16[16,256,192]{1,2,0:T(8,128)(2,1)S(1)} all-to-all(bf16[16,256,192]{1,2,0:T(8,128)(2,1)} %copy.61), channel_id=1, replica_groups=mesh['chain'=8,'dp'=16] {'dp'}, dimensions={0} | all-to-all | bytes 3145728 | tf_op jit(solution)/shard_map/all_to_all | solution.py:231
  420.7 11.0 %convolution_convert_fusion = bf16[3072,192]{0,1:T(8,128)(2,1)S(1)} fusion(bf16[4096,192]{0,1:T(8,128)(2,1)S(1)} %bitcast.30, bf16[4096,3072]{1,0:T(8,128)(2,1)} %all-gather.2.cloned.1.call-done), kind=kOutput, calls=%fused_computation | convolution fusion | flops 4832428032 | bytes 27918336 | tf_op jit(solution)/shard_map/dot_general | solution.py:232
  431.7 1.8 reshape.31
  433.5 1.8 copy.63
  435.2 4.6 all-to-all-start.1
  439.8 23.1 %all-to-all-done.1 = bf16[16,192,192]{1,2,0:T(8,128)(2,1)S(1)} async-done(((bf16[16,192,192]{1,2,0:T(8,128)(2,1)}), bf16[16,192,192]{1,2,0:T(8,128)(2,1)S(1)}, u32[]{:S(2)}, u32[]{:S(2)}) %all-to-all-start.1) | async-done | bytes 1179680 | tf_op jit(solution)/shard_map/all_to_all | solution.py:235
  462.9 2.0 bitcast_convert_fusion
  464.8 3.4 copy.64
  468.2 2.3 fusion
  471.2 1.5 copy.65
  (80 shorter events, 22.6 us)
Async XLA Ops:
  7.2 413.6 %all-gather.2.cloned.1.call-start = ((), (), s32[]{:S(2)}) async-start(), calls=%async_computation.2 | async-start | bytes 26738688 | tf_op jit(solution)/shard_map/all_gather | solution.py:228
  7.2 19.4 %copy-start.18 = (bf16[4,64,3072]{2,1,0:T(8,128)(2,1)S(1)}, bf16[4,64,3072]{2,1,0:T(8,128)(2,1)}, u32[]{:S(2)}) copy-start(bf16[4,64,3072]{2,1,0:T(8,128)(2,1)} %first_ref.21) | copy-start | bytes 4718596
  7.2 19.4 %copy-start.19 = (f32[1,3072]{1,0:T(1,128)S(1)}, f32[1,3072]{1,0:T(1,128)}, u32[]{:S(2)}) copy-start(f32[1,3072]{1,0:T(1,128)} %gain_ref.43) | copy-start | bytes 36868
  13.7 6.4 %copy-start = (bf16[3072,3072]{1,0:T(8,128)(2,1)}, bf16[3072,3072]{1,0:T(8,128)(2,1)S(1)}, u32[]{:S(2)}) copy-start(bf16[3072,3072]{1,0:T(8,128)(2,1)S(1)} %get-tuple-element.84.weight_ref) | copy-start | bytes 56623108
  20.2 6.5 %copy-start.3 = (bf16[3072,3072]{1,0:T(8,128)(2,1)}, bf16[3072,3072]{1,0:T(8,128)(2,1)S(1)}, u32[]{:S(2)}) copy-start(bf16[3072,3072]{1,0:T(8,128)(2,1)S(1)} %get-tuple-element.85.turned_in) | copy-start | bytes 56623108
  26.7 6.4 %copy-start.1 = (bf16[3072,3072]{1,0:T(8,128)(2,1)S(1)}, bf16[3072,3072]{1,0:T(8,128)(2,1)}, u32[]{:S(2)}) copy-start(bf16[3072,3072]{1,0:T(8,128)(2,1)} %copy-done) | copy-start | bytes 56623108
  33.0 6.8 %copy-start.2 = (bf16[3072,3072]{1,0:T(8,128)(2,1)S(1)}, bf16[3072,3072]{1,0:T(8,128)(2,1)}, u32[]{:S(2)}) copy-start(bf16[3072,3072]{1,0:T(8,128)(2,1)} %copy-done) | copy-start | bytes 56623108
  36.7 16.9 %collective-permute-start = (bf16[64,3072]{1,0:T(8,128)(2,1)S(1)}, bf16[64,3072]{1,0:T(8,128)(2,1)S(1)}, u32[]{:S(2)}, u32[]{:S(2)}) collective-permute-start(bf16[64,3072]{1,0:T(8,128)(2,1)S(1)} %get-tuple-element.89.after_ref), channel_id=1, source_target_pairs={{0,16},{1,25},{2,18},{3,27},{4,20},{5,29},{6,22},{7,31},{8,24},{9,... | collective-permute-start | bytes 1179656 | tf_op jit(solution)/shard_map/ppermute | solution.py:214
  39.8 6.4 %copy-start.4 = (bf16[3072,3072]{1,0:T(8,128)(2,1)S(1)}, bf16[3072,3072]{1,0:T(8,128)(2,1)}, u32[]{:S(2)}) copy-start(bf16[3072,3072]{1,0:T(8,128)(2,1)} %copy-done.3) | copy-start | bytes 56623108
  47.2 6.4 %copy-start.5 = (bf16[3072,3072]{1,0:T(8,128)(2,1)}, bf16[3072,3072]{1,0:T(8,128)(2,1)S(1)}, u32[]{:S(2)}) copy-start(bf16[3072,3072]{1,0:T(8,128)(2,1)S(1)} %get-tuple-element.90.turned_in) | copy-start | bytes 56623108
  53.6 10.8 %copy-start.6 = (bf16[3072,3072]{1,0:T(8,128)(2,1)S(1)}, bf16[3072,3072]{1,0:T(8,128)(2,1)}, u32[]{:S(2)}) copy-start(bf16[3072,3072]{1,0:T(8,128)(2,1)} %copy-done.5) | copy-start | bytes 56623108
  58.1 11.0 %collective-permute-start.1 = (bf16[64,3072]{1,0:T(8,128)(2,1)S(1)}, bf16[64,3072]{1,0:T(8,128)(2,1)S(1)}, u32[]{:S(2)}, u32[]{:S(2)}) collective-permute-start(bf16[64,3072]{1,0:T(8,128)(2,1)S(1)} %get-tuple-element.95.after_ref), channel_id=1, source_target_pairs={{0,16},{1,25},{2,18},{3,27},{4,20},{5,29},{6,22},{7,31},{8,24},{9,... | collective-permute-start | bytes 1179656 | tf_op jit(solution)/shard_map/ppermute | solution.py:214
  73.4 10.0 %collective-permute-start.2 = (bf16[64,3072]{1,0:T(8,128)(2,1)S(1)}, bf16[64,3072]{1,0:T(8,128)(2,1)S(1)}, u32[]{:S(2)}, u32[]{:S(2)}) collective-permute-start(bf16[64,3072]{1,0:T(8,128)(2,1)S(1)} %get-tuple-element.101.after_ref), channel_id=1, source_target_pairs={{0,16},{1,25},{2,18},{3,27},{4,20},{5,29},{6,22},{7,31},{8,24},{9,... | collective-permute-start | bytes 1179656 | tf_op jit(solution)/shard_map/ppermute | solution.py:214
  88.2 12.2 %collective-permute-start.3 = (bf16[64,3072]{1,0:T(8,128)(2,1)S(1)}, bf16[64,3072]{1,0:T(8,128)(2,1)S(1)}, u32[]{:S(2)}, u32[]{:S(2)}) collective-permute-start(bf16[64,3072]{1,0:T(8,128)(2,1)S(1)} %get-tuple-element.107.after_ref), channel_id=1, source_target_pairs={{0,16},{1,25},{2,18},{3,27},{4,20},{5,29},{6,22},{7,31},{8,24},{9,... | collective-permute-start | bytes 1179656 | tf_op jit(solution)/shard_map/ppermute | solution.py:214
  101.0 1.7 collective-permute-start.4
  103.3 1.7 collective-permute-start.5
  105.0 6.4 %copy-start.7 = (bf16[3072,3072]{1,0:T(8,128)(2,1)}, bf16[3072,3072]{1,0:T(8,128)(2,1)S(1)}, u32[]{:S(2)}) copy-start(bf16[3072,3072]{1,0:T(8,128)(2,1)S(1)} %get-tuple-element.141.turned_ref) | copy-start | bytes 56623108
  111.4 0.7 collective-permute-start.6
  112.1 1.5 copy-start.16
  112.9 7.8 %collective-permute-start.7 = (bf16[64,3072]{1,0:T(8,128)(2,1)S(1)}, bf16[64,3072]{1,0:T(8,128)(2,1)S(1)}, u32[]{:S(2)}, u32[]{:S(2)}) collective-permute-start(bf16[64,3072]{1,0:T(8,128)(2,1)S(1)} %get-tuple-element.128), channel_id=1, source_target_pairs={{64,80},{65,89},{66,82},{67,91},{68,84},{69,93},{70,86},{71,95},{7... | collective-permute-start | bytes 1179656 | tf_op jit(solution)/shard_map/ppermute | solution.py:214
  113.6 6.4 %copy-start.8 = (bf16[3072,3072]{1,0:T(8,128)(2,1)S(1)}, bf16[3072,3072]{1,0:T(8,128)(2,1)}, u32[]{:S(2)}) copy-start(bf16[3072,3072]{1,0:T(8,128)(2,1)} %copy-done.7) | copy-start | bytes 56623108
  120.0 2.2 collective-permute-start.10
  121.5 1.4 collective-permute-start.8
  122.2 2.0 collective-permute-start.11
  123.6 5.3 %collective-permute-start.9 = (bf16[64,3072]{1,0:T(8,128)(2,1)S(1)}, bf16[64,3072]{1,0:T(8,128)(2,1)S(1)}, u32[]{:S(2)}, u32[]{:S(2)}) collective-permute-start(bf16[64,3072]{1,0:T(8,128)(2,1)S(1)} %get-tuple-element.136), channel_id=1, source_target_pairs={{96,112},{97,121},{98,114},{99,123},{100,116},{101,125},{102,118},... | collective-permute-start | bytes 1179656 | tf_op jit(solution)/shard_map/ppermute | solution.py:214
  128.8 1.4 copy-start.12
  130.3 1.1 copy-start.10
  131.4 1.1 copy-start.15
  132.6 0.7 collective-permute-start.12
  133.3 6.4 %copy-start.9 = (bf16[3072,3072]{1,0:T(8,128)(2,1)S(1)}, bf16[3072,3072]{1,0:T(8,128)(2,1)}, u32[]{:S(2)}) copy-start(bf16[3072,3072]{1,0:T(8,128)(2,1)} %copy-done.7) | copy-start | bytes 56623108
  139.7 1.4 copy-start.11
  141.1 1.4 copy-start.13
  142.5 1.4 copy-start.17
  143.9 0.7 collective-permute-start.13
  144.8 0.7 collective-permute-start.14
  145.5 0.7 collective-permute-start.15
  146.2 130.7 %collective-permute-start.16 = (bf16[64,3072]{1,0:T(8,128)(2,1)S(1)}, bf16[64,3072]{1,0:T(8,128)(2,1)S(1)}, u32[]{:S(2)}, u32[]{:S(2)}) collective-permute-start(bf16[64,3072]{1,0:T(8,128)(2,1)S(1)} %get-tuple-element.157), channel_id=1, source_target_pairs={{16,0},{25,1},{18,2},{27,3},{20,4},{29,5},{22,6},{31,7},{24,8},{17... | collective-permute-start | bytes 1179656 | tf_op jit(solution)/shard_map/ppermute | solution.py:223
  277.7 14.1 %collective-permute-start.17 = (bf16[64,3072]{1,0:T(8,128)(2,1)S(1)}, bf16[64,3072]{1,0:T(8,128)(2,1)S(1)}, u32[]{:S(2)}, u32[]{:S(2)}) collective-permute-start(bf16[64,3072]{1,0:T(8,128)(2,1)S(1)} %get-tuple-element.159), channel_id=1, source_target_pairs={{16,0},{25,1},{18,2},{27,3},{20,4},{29,5},{22,6},{31,7},{24,8},{17... | collective-permute-start | bytes 1179656 | tf_op jit(solution)/shard_map/ppermute | solution.py:223
  292.3 15.6 %collective-permute-start.18 = (bf16[64,3072]{1,0:T(8,128)(2,1)S(1)}, bf16[64,3072]{1,0:T(8,128)(2,1)S(1)}, u32[]{:S(2)}, u32[]{:S(2)}) collective-permute-start(bf16[64,3072]{1,0:T(8,128)(2,1)S(1)} %get-tuple-element.161), channel_id=1, source_target_pairs={{16,0},{25,1},{18,2},{27,3},{20,4},{29,5},{22,6},{31,7},{24,8},{17... | collective-permute-start | bytes 1179656 | tf_op jit(solution)/shard_map/ppermute | solution.py:223
  308.5 62.7 %collective-permute-start.19 = (bf16[64,3072]{1,0:T(8,128)(2,1)S(1)}, bf16[64,3072]{1,0:T(8,128)(2,1)S(1)}, u32[]{:S(2)}, u32[]{:S(2)}) collective-permute-start(bf16[64,3072]{1,0:T(8,128)(2,1)S(1)} %get-tuple-element.163), channel_id=1, source_target_pairs={{16,0},{25,1},{18,2},{27,3},{20,4},{29,5},{22,6},{31,7},{24,8},{17... | collective-permute-start | bytes 1179656 | tf_op jit(solution)/shard_map/ppermute | solution.py:223
  372.7 1.2 copy-start.14
  435.2 27.6 %all-to-all-start.1 = ((bf16[16,192,192]{1,2,0:T(8,128)(2,1)}), bf16[16,192,192]{1,2,0:T(8,128)(2,1)S(1)}, u32[]{:S(2)}, u32[]{:S(2)}) async-start(bf16[16,192,192]{1,2,0:T(8,128)(2,1)} %copy.63), calls=%async_computation.1 | async-start | bytes 3145728 | tf_op jit(solution)/shard_map/all_to_all | solution.py:235
Sparse Core Ops, SparseCore 0:
  132.7 247.9 all-gather.1

commit v2 on v0

v2 whole, which is shorter than its diff:
```python
import functools

import jax
import jax.numpy as jnp
from jax import lax
from jax.experimental import pallas as pl
from jax.experimental.pallas import tpu as pltpu
from jax.sharding import PartitionSpec as P

SECTIONS = 8
LAST = SECTIONS - 1
TURN = 2 * LAST
REPLICAS = 16
D = 3072
SPAN = 256
SHARE = D // REPLICAS
CHIPS = REPLICAS // 2
WIDE = D // CHIPS
STREAMS = 2
SLOTS = 2
ROWS = SPAN // (STREAMS * SLOTS)
COLS = 1024
PIECES = 6
PIECE = D // PIECES
TURNED = D
INPUT = 2 * D
GRAD = INPUT + SPAN
ENDS = GRAD + SPAN
HIGH = ENDS + SPAN
LOW = HIGH + SPAN
ARENA = LOW + SPAN
COST = pl.CostEstimate(flops=2 * ROWS * D * D, bytes_accessed=4 * D * D, transcendentals=0)
VM = pl.BlockSpec(memory_space=pltpu.VMEM)
ANY = pl.BlockSpec(memory_space=pl.ANY)


def pin(array):
    return pltpu.with_memory_space_constraint(array, pltpu.VMEM)


def far(array):
    return pltpu.with_memory_space_constraint(array, pltpu.HBM)


def params(mib):
    return pltpu.CompilerParams(vmem_limit_bytes=mib << 20)


def partner(section, replica):
    z_hi, rest = divmod(replica, 8)
    core = rest % 2
    if section % 2 == 0 and core == 1:
        z_hi = 1 - z_hi
    return z_hi * 8 + rest


def route(sections, forward):
    pairs = []
    for section in sections:
        low = section if forward else section - 1
        for replica in range(REPLICAS):
            here, there = low * REPLICAS + replica, (low + 1) * REPLICAS + partner(low, replica)
            pairs.append((here, there) if forward else (there, here))
    return pairs


def inverse_rms(x_float):
    return lax.rsqrt(jnp.mean(x_float * x_float, axis=-1, keepdims=True) + 1e-06)


def at_slot(base, slot):
    return pl.ds(pl.multiple_of(base + slot * ROWS, ROWS), ROWS)


def forward_block(slot, given, gain, arena, saved, output, scaled, sem, ready=None):
    arena[at_slot(INPUT, slot)] = given
    x_float = given.astype(jnp.float32)
    scaled[...] = (x_float * inverse_rms(x_float) * gain[...]).astype(jnp.bfloat16)
    save = pltpu.make_async_copy(scaled, saved.at[at_slot(0, slot)], sem)
    save.start()
    for index, start in enumerate(range(0, D, COLS)):
        part = slice(start, start + COLS)
        if ready is not None:
            ready(index)
        hidden = jnp.dot(scaled[...], arena[0:D, part], preferred_element_type=jnp.float32)
        high = hidden.astype(jnp.bfloat16)
        arena[at_slot(HIGH, slot), part] = high
        arena[at_slot(LOW, slot), part] = (hidden - high.astype(jnp.float32)).astype(jnp.bfloat16)
        x_part = arena[at_slot(INPUT, slot), part].astype(jnp.float32)
        output[:, part] = (x_part + jax.nn.gelu(hidden)).astype(jnp.bfloat16)
    save.wait()


def first_kernel(weight, tokens, cotangent, gain, output, arena, saved, scaled, sems):
    section = lax.axis_index("chain")
    ends = arena.at[pl.ds(ENDS, SPAN)]
    load_tokens = pltpu.make_async_copy(tokens, ends, sems.at[1])
    load_cotangent = pltpu.make_async_copy(cotangent, ends, sems.at[1])
    parts = [
        pltpu.make_async_copy(
            weight.at[:, pl.ds(start, COLS)], arena.at[pl.ds(0, D), pl.ds(start, COLS)], sems.at[2 + index]
        )
        for index, start in enumerate(range(0, D, COLS))
    ]
    @pl.when(section == 0)
    def _():
        load_tokens.start()

    for part in parts:
        part.start()

    @pl.when(section == LAST)
    def _():
        load_cotangent.start()

    @pl.when(section == 0)
    def _():
        load_tokens.wait()
        given = arena[ENDS : ENDS + ROWS]
        forward_block(
            0, given, gain, arena, saved, output, scaled, sems.at[0], lambda index: parts[index].wait()
        )

    @pl.when(section != 0)
    def _():
        for part in parts:
            part.wait()

    @pl.when(section == LAST)
    def _():
        load_cotangent.wait()


def first(weight, tokens, cotangent, gain):
    return pl.pallas_call(
        first_kernel,
        out_shape=[
            jax.ShapeDtypeStruct((ROWS, D), jnp.bfloat16),
            pltpu.VMEM((ARENA, D), jnp.bfloat16),
            jax.ShapeDtypeStruct((SPAN, D), jnp.bfloat16),
        ],
        in_specs=[ANY] * 3 + [VM],
        out_specs=[VM, VM, ANY],
        scratch_shapes=[pltpu.VMEM((ROWS, D), jnp.bfloat16), pltpu.SemaphoreType.DMA((2 + D // COLS,))],
        name="load_and_first_block",
        cost_estimate=COST,
        compiler_params=params(12),
    )(far(weight), far(tokens), far(cotangent), gain)


def turn_piece(piece, arena):
    step = 256
    for offset in range(0, PIECE, step):
        start = pl.multiple_of(piece * PIECE + offset, step)
        arena[TURNED : TURNED + D, pl.ds(start, step)] = arena[pl.ds(start, step), :].T


def forward_kernel(moment, stream, *refs):
    given_ref = refs[0] if moment else None
    gain, _, _, output, arena, saved, scaled, sem = refs[-8:]
    section = lax.axis_index("chain")
    place = moment - section
    active = jnp.logical_and(place >= 0, place < SLOTS)

    @pl.when(active)
    def _():
        start = ENDS + (stream * SLOTS + moment) * ROWS
        if moment == 0:
            given = arena[start : start + ROWS]
        elif moment < SLOTS:
            given = jnp.where(section == 0, arena[start : start + ROWS], given_ref[...])
        else:
            given = given_ref[...]
        forward_block(stream * SLOTS + place, given, gain, arena, saved, output, scaled, sem)

    if stream == STREAMS - 1 and moment < PIECES + SLOTS:
        piece = jnp.where(place < 0, moment, moment - SLOTS)

        @pl.when(jnp.logical_and(jnp.logical_not(active), piece < PIECES))
        def _():
            turn_piece(piece, arena)


def forward(moment, stream, given, gain, arena, saved):
    given = [given] if moment else []
    return pl.pallas_call(
        functools.partial(forward_kernel, moment, stream),
        out_shape=[
            jax.ShapeDtypeStruct((ROWS, D), jnp.bfloat16),
            jax.ShapeDtypeStruct(arena.shape, arena.dtype),
            jax.ShapeDtypeStruct(saved.shape, saved.dtype),
        ],
        in_specs=[VM] * (2 + len(given)) + [ANY],
        out_specs=[VM, VM, ANY],
        input_output_aliases={1 + len(given): 1, 2 + len(given): 2},
        scratch_shapes=[pltpu.VMEM((ROWS, D), jnp.bfloat16), pltpu.SemaphoreType.DMA],
        name=f"forward_{moment}_{stream}",
        cost_estimate=COST,
        compiler_params=params(6),
    )(*given, gain, pin(arena), saved)


def backward_kernel(moment, stream, held, pack, *refs):
    given_ref = refs[0] if moment > LAST else None
    gain = refs[0 if moment == LAST else 1]
    output, arena = refs[len(refs) - held - pack - 2 : len(refs) - held - pack]
    section = lax.axis_index("chain")
    place = moment - TURN + section
    slot = stream * SLOTS + place

    def upstream(part):
        start = ENDS + (stream * SLOTS + moment - LAST) * ROWS
        if moment == LAST:
            given = arena[start : start + ROWS, part]
        elif moment - LAST < SLOTS:
            given = jnp.where(section == LAST, arena[start : start + ROWS, part], given_ref[:, part])
        else:
            given = given_ref[:, part]
        return given.astype(jnp.float32)

    @pl.when(jnp.logical_and(place >= 0, place < SLOTS))
    def _():
        total = jnp.zeros((ROWS, 1), jnp.float32)
        for start in range(0, D, COLS):
            part = slice(start, start + COLS)
            high = arena[at_slot(HIGH, slot), part].astype(jnp.float32)
            hidden = high + arena[at_slot(LOW, slot), part].astype(jnp.float32)
            _, pullback = jax.vjp(jax.nn.gelu, hidden)
            grad_hidden = pullback(upstream(part))[0].astype(jnp.bfloat16)
            arena[at_slot(GRAD, slot), part] = grad_hidden
            total = total + jnp.sum(grad_hidden.astype(jnp.float32) * hidden, axis=-1, keepdims=True)

        @pl.when(section > 0)
        def _():
            inv_rms = inverse_rms(arena[at_slot(INPUT, slot)].astype(jnp.float32))
            mean = total * (1.0 / D)
            for start in range(0, D, COLS):
                part = slice(start, start + COLS)
                grad_normed = gain[:, part] * jnp.dot(
                    arena[at_slot(GRAD, slot)],
                    arena[TURNED : TURNED + D, part],
                    preferred_element_type=jnp.float32,
                )
                normed = arena[at_slot(INPUT, slot), part].astype(jnp.float32) * inv_rms
                grad_input = upstream(part) + inv_rms * (grad_normed - normed * mean)
                output[:, part] = grad_input.astype(jnp.bfloat16)

    if pack:
        packed = refs[-1]
        for chip in range(CHIPS):
            packed[chip] = arena[GRAD : GRAD + SPAN, chip * WIDE : (chip + 1) * WIDE].T


def backward(moment, stream, given, gain, arena, held, pack):
    given = [given] if moment > LAST else []
    count = len(given)
    return pl.pallas_call(
        functools.partial(backward_kernel, moment, stream, len(held), int(pack)),
        out_shape=[
            jax.ShapeDtypeStruct((ROWS, D), jnp.bfloat16),
            jax.ShapeDtypeStruct(arena.shape, arena.dtype),
        ]
        + [jax.ShapeDtypeStruct(a.shape, a.dtype) for a in held]
        + [jax.ShapeDtypeStruct((CHIPS, WIDE, SPAN), jnp.bfloat16)] * pack,
        in_specs=[VM] * (2 + count) + [ANY] * len(held),
        out_specs=[VM, VM] + [ANY] * len(held) + [VM] * pack,
        input_output_aliases={1 + count + i: 1 + i for i in range(1 + len(held))},
        name=f"backward_{moment}_{stream}",
        cost_estimate=COST,
        compiler_params=params(6),
    )(*given, gain, pin(arena), *held)


def product_kernel(grads, *refs):
    pieces, (keep, give, held, total, sems) = refs[:CHIPS], refs[CHIPS:]
    replica = lax.axis_index("dp")
    z_hi, y, core = replica // 8, (replica // 2) % 4, replica % 2
    loads = [pltpu.make_async_copy(piece, held.at[i], sems.at[i]) for i, piece in enumerate(pieces)]
    for load in loads:
        load.start()
    for index, (flip, turn) in enumerate(PIECE_FROM):
        chip = (z_hi if flip == 0 else 1 - z_hi) * 4 + (y + turn) % 4
        loads[index].wait()
        for start in range(0, D, COLS):
            part = slice(start, start + COLS)
            term = jnp.dot(grads[chip], held[index, :, part], preferred_element_type=jnp.float32)
            total[:, part] = term if index == 0 else total[:, part] + term
    for chip in range(CHIPS):
        turned = total[:, chip * WIDE : (chip + 1) * WIDE].T
        low, high = turned[:SHARE], turned[SHARE:]
        keep[chip] = jnp.where(core == 0, low, high)
        give[chip] = jnp.where(core == 0, high, low).astype(jnp.bfloat16)


def product(grads, pieces):
    block = (CHIPS, SHARE, WIDE)
    return pl.pallas_call(
        product_kernel,
        out_shape=[jax.ShapeDtypeStruct(block, jnp.float32), jax.ShapeDtypeStruct(block, jnp.bfloat16)],
        in_specs=[VM] + [ANY] * CHIPS,
        out_specs=[VM, VM],
        scratch_shapes=[
            pltpu.VMEM((CHIPS, SPAN, D), jnp.bfloat16),
            pltpu.VMEM((WIDE, D), jnp.float32),
            pltpu.SemaphoreType.DMA((CHIPS,)),
        ],
        name="weight_product",
        compiler_params=params(36),
    )(grads, *pieces)


def add_kernel(keep, taken, whole):
    whole[...] = (keep[...] + taken[...].astype(jnp.float32)).astype(jnp.bfloat16)


def add(keep, taken):
    return pl.pallas_call(
        add_kernel,
        out_shape=jax.ShapeDtypeStruct(taken.shape, taken.dtype),
        in_specs=[VM, VM],
        out_specs=VM,
        name="add_cores",
        compiler_params=params(24),
    )(keep, taken)


def finish_kernel(blocks, weight, gain, rows_ref, gain_ref, own, sem):
    start = pl.multiple_of(lax.axis_index("dp") * SHARE, SHARE)
    load = pltpu.make_async_copy(weight.at[pl.ds(start, SHARE)], own, sem)
    load.start()
    for chip in range(CHIPS):
        rows_ref[:, chip * WIDE : (chip + 1) * WIDE] = blocks[chip]
    load.wait()
    total = jnp.zeros((SHARE, 1), jnp.float32)
    for chip in range(CHIPS):
        part = slice(chip * WIDE, (chip + 1) * WIDE)
        term = own[:, part].astype(jnp.float32) * blocks[chip].astype(jnp.float32)
        total = total + jnp.sum(term, axis=-1, keepdims=True)
    gain_ref[...] = total


def finish(blocks, weight, gain):
    return pl.pallas_call(
        finish_kernel,
        out_shape=[
            jax.ShapeDtypeStruct((SHARE, D), jnp.bfloat16),
            jax.ShapeDtypeStruct((SHARE, 1), jnp.float32),
        ],
        in_specs=[VM, ANY, VM],
        out_specs=[VM, VM],
        scratch_shapes=[pltpu.VMEM((SHARE, D), jnp.bfloat16), pltpu.SemaphoreType.DMA],
        name="weight_rows",
        compiler_params=params(12),
    )(blocks, far(weight), gain)


PIECE_FROM = ((0, 0), (0, 3), (0, 1), (1, 0), (1, 3), (1, 1), (0, 2), (1, 2))


def along(flip, turn):
    pairs = []
    for replica in range(REPLICAS):
        z_hi, y, core = replica // 8, (replica // 2) % 4, replica % 2
        source = (z_hi ^ flip) * 8 + (y + turn) % 4 * 2 + core
        pairs.append((source, replica))
    return pairs


def bring(array, flip, turn):
    return lax.ppermute(array, "dp", along(flip, turn))


def on_device(tokens, cotangent, weights, gains):
    axes = ("chain", "dp")
    output, arena, saved = first(
        weights[0], tokens.reshape(SPAN, D), cotangent.reshape(SPAN, D), gains
    )
    arriving = [None] * STREAMS
    returning = [None] * STREAMS
    pieces = {}
    for moment in range(TURN + SLOTS):
        sent = list(arriving)
        for stream in range(STREAMS):
            if moment < LAST + SLOTS:
                if moment or stream:
                    output, arena, saved = forward(
                        moment, stream, arriving[stream], gains, arena, saved
                    )
                senders = [s for s in range(LAST) if 0 <= moment - s < SLOTS]
                if senders:
                    sent[stream] = lax.ppermute(output, axes, route(senders, True))
            if moment >= LAST:
                held = HELD.get((moment, stream), ())
                output, arena, *through = backward(
                    moment, stream, returning[stream], gains, arena, [pieces[name] for name in held],
                    (moment, stream) == (TURN + SLOTS - 1, STREAMS - 1),
                )
                pieces.update(zip(held, through))
                packed = through[-1:]
                senders = [s for s in range(1, SECTIONS) if 0 <= moment - TURN + s < SLOTS]
                if senders:
                    returning[stream] = lax.ppermute(output, axes, route(senders, False))
            if (moment, stream) == (LAST + SLOTS - 1, STREAMS - 1):
                pieces[0, 0] = saved
                pieces[1, 0] = bring(saved, 1, 0)
                pieces[0, 3] = bring(saved, 0, 3)
                pieces[0, 1] = bring(saved, 0, 1)
            if (moment, stream) == FLIPPED:
                pieces[1, 3] = bring(pieces[1, 0], 0, 3)
                pieces[1, 1] = bring(pieces[1, 0], 0, 1)
            if (moment, stream) == FAR:
                pieces[0, 2] = bring(pieces[0, 3], 0, 3)
                pieces[1, 2] = bring(pieces[1, 1], 0, 1)
        arriving = sent

    chips = [[replica for replica in range(REPLICAS) if replica % 2 == core] for core in range(2)]
    columns = lax.all_to_all(packed[0], "dp", 0, 0, axis_index_groups=chips)
    keep, give = product(columns, [pieces[name] for name in PIECE_FROM])
    other = [(replica ^ 1, replica) for replica in range(REPLICAS)]
    blocks = add(keep, lax.ppermute(give, "dp", other))
    blocks = lax.all_to_all(blocks, "dp", 0, 0, axis_index_groups=chips)
    weight_rows, sums = finish(blocks, weights[0], gains)
    own_gain = lax.dynamic_slice_in_dim(gains[0], lax.axis_index("dp") * SHARE, SHARE, 0)
    return (weight_rows[None], (sums[:, 0] / own_gain)[None])


FLIPPED = (LAST + SLOTS + 1, 1)
FAR = (LAST + SLOTS + 4, 1)
HELD = {FLIPPED: ((1, 0),), FAR: ((0, 3), (1, 1))}


def solution(mesh):
    placed = (P(None, "dp", None), P(None, "dp", None), P("chain", None, None), P("chain", None))
    return jax.shard_map(
        on_device,
        mesh=mesh,
        in_specs=placed,
        out_specs=(P("chain", "dp", None), P("chain", "dp")),
        check_vma=False,
    )
```

time: 800 us -> 486 us (0.61)
  the two profiles are of different devices: /device:TPU:1 before, /device:TPU:32 now
where the time goes in v2:
time: 486 us; the launch traced here: 478 us
  waiting for transfers between devices  204 us (42%)
  starting transfers between devices  126 us (26%)
  Pallas kernels  113 us (23%)
  local copies, waits for them, and re-layouts  32.9 us (7%)
    ppermute x16, waiting for transfers between devices, on_device(): returning[stream] = lax.ppermute(output, axes, route(senders, False))  82.9 us
    ppermute x7, waiting for transfers between devices, bring(): return lax.ppermute(array, 'dp', along(flip, turn))  81 us
    ppermute x7, starting transfers between devices, bring(): return lax.ppermute(array, 'dp', along(flip, turn))  77 us
    pallas_call x18, Pallas kernels, backward(): pl.pallas_call(functools.partial(backward_kernel, moment, stream, len(hel...  60.1 us
    unnamed x14, local copies, waits for them, and re-layouts  32.9 us
    pallas_call x17, Pallas kernels, forward(): pl.pallas_call(functools.partial(forward_kernel, moment, stream), out_sha...  32 us
    ppermute x16, starting transfers between devices, on_device(): sent[stream] = lax.ppermute(output, axes, route(senders, True))  20.4 us
    all_to_all x1, waiting for transfers between devices, on_device(): blocks = lax.all_to_all(blocks, 'dp', 0, 0, axis_index_groups=chips)  18.9 us
  transfers between devices with their start and end apart: 42, of which 13 were waited for; matrix products, arithmetic and copies ran while one was open for 0% of the time, Pallas kernels for 19%

profile of v2, /device:TPU:32, one launch (start us, length us, event | category | flops | bytes accessed | tf_op | source)
XLA Modules:
  0.0 478.2 jit_solution(15479032768129158796)
XLA Ops:
  0.6 8.0 %load_and_first_block.1 = (bf16[64,3072]{1,0:T(8,128)(2,1)}, bf16[7424,3072]{1,0:T(8,128)(2,1)S(1)}, bf16[256,3072]{1,0:T(8,128)(2,1)}) custom-call(bf16[3072,3072]{1,0:T(8,128)(2,1)} %bitcast.5, bf16[256,3072]{1,0:T(8,128)(2,1)} %bitcast.7, bf16[256,3072]{1,0:T(8,128)(2,1)} %bitcast.8, f32[1,3072]{1,0:T(1,128)} %gain.3), custom_call_target="tpu_custom_call" | custom-call | flops 1207959552 | bytes 37748736 | tf_op jit(solution)/shard_map/load_and_first_block/pallas_call | solution.py:135
  8.6 15.0 %copy-done = bf16[7424,3072]{1,0:T(8,128)(2,1)} copy-done((bf16[7424,3072]{1,0:T(8,128)(2,1)}, bf16[7424,3072]{1,0:T(8,128)(2,1)S(1)}, u32[]{:S(2)}) %copy-start) | copy-done | bytes 45613080
  25.0 14.1 %copy-done.1 = bf16[7424,3072]{1,0:T(8,128)(2,1)S(1)} copy-done((bf16[7424,3072]{1,0:T(8,128)(2,1)S(1)}, bf16[7424,3072]{1,0:T(8,128)(2,1)}, u32[]{:S(2)}) %copy-start.1) | copy-done | bytes 45613080
  39.0 1.4 copy-done.2
  41.5 1.3 collective-permute-start
  42.8 4.4 forward_1_0.1
  47.2 1.9 collective-permute-start.3
  49.1 5.4 %collective-permute-done.refs_0_ = bf16[64,3072]{1,0:T(8,128)(2,1)S(1)} collective-permute-done((bf16[64,3072]{1,0:T(8,128)(2,1)S(1)}, bf16[64,3072]{1,0:T(8,128)(2,1)S(1)}, u32[]{:S(2)}, u32[]{:S(2)}) %collective-permute-start) | collective-permute-done | bytes 393248 | tf_op jit(solution)/shard_map/ppermute | solution.py:391
  54.5 4.8 %forward_1_1.1 = (bf16[64,3072]{1,0:T(8,128)(2,1)S(1)}, bf16[7424,3072]{1,0:T(8,128)(2,1)S(1)}, bf16[256,3072]{1,0:T(8,128)(2,1)S(1)}) custom-call(bf16[64,3072]{1,0:T(8,128)(2,1)S(1)} %collective-permute-done.refs_0_, f32[1,3072]{1,0:T(1,128)S(1)} %copy-done.5, ...), custom_call_target="tpu_custom_call", output_to_operand_aliasing={{1}: (2, {}), {2}: (3, {})} | custom-call | flops 1207959552 | bytes 37748736 | tf_op jit(solution)/shard_map/forward_1_1/pallas_call | solution.py:186
  59.3 1.9 collective-permute-start.2
  61.2 4.4 forward_2_0.1
  65.6 1.8 collective-permute-start.5
  67.4 3.2 collective-permute-done.2.refs_0_
  70.6 4.3 forward_2_1.1
  75.0 5.3 %collective-permute-start.4 = (bf16[64,3072]{1,0:T(8,128)(2,1)S(1)}, bf16[64,3072]{1,0:T(8,128)(2,1)S(1)}, u32[]{:S(2)}, u32[]{:S(2)}) collective-permute-start(bf16[64,3072]{1,0:T(8,128)(2,1)S(1)} %get-tuple-element.109), channel_id=1, source_target_pairs={{16,32},{17,33},{18,34},{19,35},{20,36},{21,37},{22,38},{23,39},{2... | collective-permute-start | bytes 1179656 | tf_op jit(solution)/shard_map/ppermute | solution.py:391
  81.2 6.7 %collective-permute-done.4.refs_0_ = bf16[64,3072]{1,0:T(8,128)(2,1)S(1)} collective-permute-done((bf16[64,3072]{1,0:T(8,128)(2,1)S(1)}, bf16[64,3072]{1,0:T(8,128)(2,1)S(1)}, u32[]{:S(2)}, u32[]{:S(2)}) %collective-permute-start.4) | collective-permute-done | bytes 393248 | tf_op jit(solution)/shard_map/ppermute | solution.py:391
  94.9 5.8 %forward_6_0.1 = (bf16[64,3072]{1,0:T(8,128)(2,1)S(1)}, bf16[7424,3072]{1,0:T(8,128)(2,1)S(1)}, bf16[256,3072]{1,0:T(8,128)(2,1)S(1)}) custom-call(bf16[64,3072]{1,0:T(8,128)(2,1)S(1)} %collective-permute-done.11.refs_0_, f32[1,3072]{1,0:T(1,128)S(1)} %copy-done.5, ...), custom_call_target="tpu_custom_call", output_to_operand_aliasing={{1}: (2, {}), {2}: (3, {})} | custom-call | flops 1207959552 | bytes 37748736 | tf_op jit(solution)/shard_map/forward_6_0/pallas_call | solution.py:186
  105.1 3.8 backward_7_0.1
  112.1 8.4 %backward_8_0.1 = (bf16[64,3072]{1,0:T(8,128)(2,1)S(1)}, bf16[7424,3072]{1,0:T(8,128)(2,1)S(1)}) custom-call(bf16[64,3072]{1,0:T(8,128)(2,1)S(1)} %collective-permute-done.16.refs_0_, f32[1,3072]{1,0:T(1,128)S(1)} %copy-done.5, bf16[7424,3072]{1,0:T(8,128)(2,1)S(1)} %get-tuple-element.147.refs_2_), custom_call_target="tpu_custom_call", output_to_operand_aliasing={{1}: (2, {})} | custom-call | flops 1207959552 | bytes 37748736 | tf_op jit(solution)/shard_map/backward_8_0/pallas_call | solution.py:257
  121.3 65.4 %collective-permute-start.22 = (bf16[256,3072]{1,0:T(8,128)(2,1)S(1)}, bf16[256,3072]{1,0:T(8,128)(2,1)S(1)}, u32[]{:S(2)}, u32[]{:S(2)}) collective-permute-start(bf16[256,3072]{1,0:T(8,128)(2,1)S(1)} %get-tuple-element.159.refs_0_), channel_id=1, source_target_pairs={{8,0},{9,1},{10,2},{11,3},{12,4},{13,5},{14,6},{15,7},{0,8},{1,9},... | collective-permute-start | bytes 4718600 | tf_op jit(solution)/shard_map/ppermute | solution.py:370
  189.6 8.6 %backward_9_1.1 = (bf16[64,3072]{1,0:T(8,128)(2,1)S(1)}, bf16[7424,3072]{1,0:T(8,128)(2,1)S(1)}) custom-call(bf16[64,3072]{1,0:T(8,128)(2,1)S(1)} %collective-permute-done.18.refs_0_, f32[1,3072]{1,0:T(1,128)S(1)} %copy-done.5, bf16[7424,3072]{1,0:T(8,128)(2,1)S(1)} %get-tuple-element.154.refs_2_), custom_call_target="tpu_custom_call", output_to_operand_aliasing={{1}: (2, {})} | custom-call | flops 1207959552 | bytes 37748736 | tf_op jit(solution)/shard_map/backward_9_1/pallas_call | solution.py:257
  198.9 1.6 collective-permute-start.29
  200.5 23.6 %collective-permute-done.22.refs_3_ = bf16[256,3072]{1,0:T(8,128)(2,1)S(1)} collective-permute-done((bf16[256,3072]{1,0:T(8,128)(2,1)S(1)}, bf16[256,3072]{1,0:T(8,128)(2,1)S(1)}, u32[]{:S(2)}, u32[]{:S(2)}) %collective-permute-start.22) | collective-permute-done | bytes 1572896 | tf_op jit(solution)/shard_map/ppermute | solution.py:370
  224.1 2.9 collective-permute-start.30
  229.1 8.4 %backward_11_1.1 = (bf16[64,3072]{1,0:T(8,128)(2,1)S(1)}, bf16[7424,3072]{1,0:T(8,128)(2,1)S(1)}) custom-call(bf16[64,3072]{1,0:T(8,128)(2,1)S(1)} %collective-permute-done.23.refs_0_, f32[1,3072]{1,0:T(1,128)S(1)} %copy-done.5, bf16[7424,3072]{1,0:T(8,128)(2,1)S(1)} %get-tuple-element.163.refs_2_), custom_call_target="tpu_custom_call", output_to_operand_aliasing={{1}: (2, {})} | custom-call | flops 1207959552 | bytes 37748736 | tf_op jit(solution)/shard_map/backward_11_1/pallas_call | solution.py:257
  240.9 71.1 %collective-permute-done.28.refs_0_ = bf16[64,3072]{1,0:T(8,128)(2,1)S(1)} collective-permute-done((bf16[64,3072]{1,0:T(8,128)(2,1)S(1)}, bf16[64,3072]{1,0:T(8,128)(2,1)S(1)}, u32[]{:S(2)}, u32[]{:S(2)}) %collective-permute-start.28) | collective-permute-done | bytes 393248 | tf_op jit(solution)/shard_map/ppermute | solution.py:402
  312.0 4.4 backward_13_0.1
  316.4 1.9 collective-permute-start.32
  318.3 7.1 %collective-permute-done.27.refs_0_ = bf16[64,3072]{1,0:T(8,128)(2,1)S(1)} collective-permute-done((bf16[64,3072]{1,0:T(8,128)(2,1)S(1)}, bf16[64,3072]{1,0:T(8,128)(2,1)S(1)}, u32[]{:S(2)}, u32[]{:S(2)}) %collective-permute-start.27) | collective-permute-done | bytes 393248 | tf_op jit(solution)/shard_map/ppermute | solution.py:402
  325.4 8.2 %backward_13_1.1 = (bf16[64,3072]{1,0:T(8,128)(2,1)S(1)}, bf16[7424,3072]{1,0:T(8,128)(2,1)S(1)}, bf16[256,3072]{1,0:T(8,128)(2,1)}, bf16[256,3072]{1,0:T(8,128)(2,1)}) custom-call(bf16[64,3072]{1,0:T(8,128)(2,1)S(1)} %collective-permute-done.27.refs_0_, f32[1,3072]{1,0:T(1,128)S(1)} %copy-done.5, ...), custom_call_target="tpu_custom_call", output_to_operand_aliasing={{1}: (2, {}), {2}: (3, {}), {3}: (4, {})} | custom-call | flops 1207959552 | bytes 37748736 | tf_op jit(solution)/shard_map/backward_13_1/pallas_call | solution.py:257
  333.6 1.9 collective-permute-start.31
  335.5 4.4 backward_14_0.1
  339.9 1.3 collective-permute-start.34
  341.2 4.6 collective-permute-done.31.refs_0_
  345.9 4.4 backward_14_1.1
  350.3 1.3 collective-permute-start.33
  353.7 5.0 %collective-permute-start.38 = (bf16[256,3072]{1,0:T(8,128)(2,1)}, bf16[256,3072]{1,0:T(8,128)(2,1)}, u32[]{:S(2)}, u32[]{:S(2)}) collective-permute-start(bf16[256,3072]{1,0:T(8,128)(2,1)} %get-tuple-element.183.refs_5_), channel_id=1, source_target_pairs={{2,0},{3,1},{4,2},{5,3},{6,4},{7,5},{0,6},{1,7},{10,8},{11,9},{12,... | collective-permute-start | bytes 4718600 | tf_op jit(solution)/shard_map/ppermute | solution.py:370
  358.7 8.7 %backward_15_0.1 = (bf16[64,3072]{1,0:T(8,128)(2,1)}, bf16[7424,3072]{1,0:T(8,128)(2,1)S(1)}) custom-call(bf16[64,3072]{1,0:T(8,128)(2,1)S(1)} %collective-permute-done.34.refs_0_, f32[1,3072]{1,0:T(1,128)S(1)} %copy-done.5, bf16[7424,3072]{1,0:T(8,128)(2,1)S(1)} %get-tuple-element.179.refs_2_), custom_call_target="tpu_custom_call", output_to_operand_aliasing={{1}: (2, {})} | custom-call | flops 1207959552 | bytes 37748736 | tf_op jit(solution)/shard_map/backward_15_0/pallas_call | solution.py:257
  369.4 6.4 %all-to-all-start = ((bf16[8,384,256]{2,1,0:T(8,128)(2,1)}), bf16[8,384,256]{2,1,0:T(8,128)(2,1)}, u32[]{:S(2)}, u32[]{:S(2)}) async-start(bf16[8,384,256]{2,1,0:T(8,128)(2,1)} %copy-done.6), calls=%async_computation | async-start | bytes 3145728 | tf_op jit(solution)/shard_map/all_to_all | solution.py:417
  375.8 13.3 %collective-permute-done.35.refs_2_ = bf16[256,3072]{1,0:T(8,128)(2,1)} collective-permute-done((bf16[256,3072]{1,0:T(8,128)(2,1)S(1)}, bf16[256,3072]{1,0:T(8,128)(2,1)}, u32[]{:S(2)}, u32[]{:S(2)}) %collective-permute-start.35) | collective-permute-done | bytes 1572896 | tf_op jit(solution)/shard_map/ppermute | solution.py:370
  389.1 2.0 collective-permute-done.36.refs_4_
  391.1 42.1 %collective-permute-done.37.refs_6_ = bf16[256,3072]{1,0:T(8,128)(2,1)} collective-permute-done((bf16[256,3072]{1,0:T(8,128)(2,1)}, bf16[256,3072]{1,0:T(8,128)(2,1)}, u32[]{:S(2)}, u32[]{:S(2)}) %collective-permute-start.37) | collective-permute-done | bytes 1572896 | tf_op jit(solution)/shard_map/ppermute | solution.py:370
  433.2 2.9 all-to-all-done.grads
  436.1 9.4 %weight_product.1 = (f32[8,192,384]{2,1,0:T(8,128)S(1)}, bf16[8,192,384]{2,1,0:T(8,128)(2,1)S(1)}) custom-call(bf16[8,384,256]{2,1,0:T(8,128)(2,1)} %all-to-all-done.grads, bf16[256,3072]{1,0:T(8,128)(2,1)S(1)} %get-tuple-element.159.refs_0_, bf16[256,3072]{1,0:T(8,128)(2,1)} %get-tuple-element.182.refs_1_, ...), custom_call_target="tpu_custom_call" | custom-call | tf_op jit(solution)/shard_map/weight_product/pallas_call | solution.py:297
  445.6 2.8 collective-permute-done.39.taken
  449.7 6.0 %all-to-all-start.1 = ((bf16[8,192,384]{2,1,0:T(8,128)(2,1)}), bf16[8,192,384]{2,1,0:T(8,128)(2,1)S(1)}, u32[]{:S(2)}, u32[]{:S(2)}) async-start(bf16[8,192,384]{2,1,0:T(8,128)(2,1)} %add_cores.1), calls=%async_computation.1 | async-start | bytes 2359296 | tf_op jit(solution)/shard_map/all_to_all | solution.py:421
  455.7 18.9 %all-to-all-done.1.blocks = bf16[8,192,384]{2,1,0:T(8,128)(2,1)S(1)} async-done(((bf16[8,192,384]{2,1,0:T(8,128)(2,1)}), bf16[8,192,384]{2,1,0:T(8,128)(2,1)S(1)}, u32[]{:S(2)}, u32[]{:S(2)}) %all-to-all-start.1) | async-done | bytes 1179680 | tf_op jit(solution)/shard_map/all_to_all | solution.py:421
  474.6 2.6 weight_rows.1
  (91 shorter events, 33.4 us)
Async XLA Ops:
  0.6 24.3 %copy-start.5 = (f32[1,3072]{1,0:T(1,128)S(1)}, f32[1,3072]{1,0:T(1,128)}, u32[]{:S(2)}) copy-start(f32[1,3072]{1,0:T(1,128)} %gain.3) | copy-start | bytes 36868
  8.6 15.0 %copy-start = (bf16[7424,3072]{1,0:T(8,128)(2,1)}, bf16[7424,3072]{1,0:T(8,128)(2,1)S(1)}, u32[]{:S(2)}) copy-start(bf16[7424,3072]{1,0:T(8,128)(2,1)S(1)} %get-tuple-element.95.refs_1_) | copy-start | bytes 136839168
  23.7 19.1 %collective-permute-start.1 = (bf16[64,3072]{1,0:T(8,128)(2,1)}, bf16[64,3072]{1,0:T(8,128)(2,1)S(1)}, u32[]{:S(2)}, u32[]{:S(2)}) collective-permute-start(bf16[64,3072]{1,0:T(8,128)(2,1)} %get-tuple-element.98), channel_id=1, source_target_pairs={{0,16},{1,25},{2,18},{3,27},{4,20},{5,29},{6,22},{7,31},{8,24},{9,... | collective-permute-start | bytes 1179656 | tf_op jit(solution)/shard_map/ppermute | solution.py:391
  25.0 14.1 %copy-start.1 = (bf16[7424,3072]{1,0:T(8,128)(2,1)S(1)}, bf16[7424,3072]{1,0:T(8,128)(2,1)}, u32[]{:S(2)}) copy-start(bf16[7424,3072]{1,0:T(8,128)(2,1)} %copy-done) | copy-start | bytes 136839168
  39.0 1.4 copy-start.2
  41.5 13.0 %collective-permute-start = (bf16[64,3072]{1,0:T(8,128)(2,1)S(1)}, bf16[64,3072]{1,0:T(8,128)(2,1)S(1)}, u32[]{:S(2)}, u32[]{:S(2)}) collective-permute-start(bf16[64,3072]{1,0:T(8,128)(2,1)S(1)} %get-tuple-element.97), channel_id=1, source_target_pairs={{0,16},{1,25},{2,18},{3,27},{4,20},{5,29},{6,22},{7,31},{8,24},{9,... | collective-permute-start | bytes 1179656 | tf_op jit(solution)/shard_map/ppermute | solution.py:391
  47.2 14.0 %collective-permute-start.3 = (bf16[64,3072]{1,0:T(8,128)(2,1)S(1)}, bf16[64,3072]{1,0:T(8,128)(2,1)S(1)}, u32[]{:S(2)}, u32[]{:S(2)}) collective-permute-start(bf16[64,3072]{1,0:T(8,128)(2,1)S(1)} %get-tuple-element.104), channel_id=1, source_target_pairs={{0,16},{1,25},{2,18},{3,27},{4,20},{5,29},{6,22},{7,31},{8,24},{9,... | collective-permute-start | bytes 1179656 | tf_op jit(solution)/shard_map/ppermute | solution.py:391
  59.3 11.3 %collective-permute-start.2 = (bf16[64,3072]{1,0:T(8,128)(2,1)S(1)}, bf16[64,3072]{1,0:T(8,128)(2,1)S(1)}, u32[]{:S(2)}, u32[]{:S(2)}) collective-permute-start(bf16[64,3072]{1,0:T(8,128)(2,1)S(1)} %get-tuple-element.103), channel_id=1, source_target_pairs={{0,16},{1,25},{2,18},{3,27},{4,20},{5,29},{6,22},{7,31},{8,24},{9,... | collective-permute-start | bytes 1179656 | tf_op jit(solution)/shard_map/ppermute | solution.py:391
  65.6 14.7 %collective-permute-start.5 = (bf16[64,3072]{1,0:T(8,128)(2,1)S(1)}, bf16[64,3072]{1,0:T(8,128)(2,1)S(1)}, u32[]{:S(2)}, u32[]{:S(2)}) collective-permute-start(bf16[64,3072]{1,0:T(8,128)(2,1)S(1)} %get-tuple-element.110), channel_id=1, source_target_pairs={{16,32},{17,33},{18,34},{19,35},{20,36},{21,37},{22,38},{23,39},{2... | collective-permute-start | bytes 1179656 | tf_op jit(solution)/shard_map/ppermute | solution.py:391
  75.0 13.0 %collective-permute-start.4 = (bf16[64,3072]{1,0:T(8,128)(2,1)S(1)}, bf16[64,3072]{1,0:T(8,128)(2,1)S(1)}, u32[]{:S(2)}, u32[]{:S(2)}) collective-permute-start(bf16[64,3072]{1,0:T(8,128)(2,1)S(1)} %get-tuple-element.109), channel_id=1, source_target_pairs={{16,32},{17,33},{18,34},{19,35},{20,36},{21,37},{22,38},{23,39},{2... | collective-permute-start | bytes 1179656 | tf_op jit(solution)/shard_map/ppermute | solution.py:391
  80.5 9.2 %collective-permute-start.7 = (bf16[64,3072]{1,0:T(8,128)(2,1)S(1)}, bf16[64,3072]{1,0:T(8,128)(2,1)S(1)}, u32[]{:S(2)}, u32[]{:S(2)}) collective-permute-start(bf16[64,3072]{1,0:T(8,128)(2,1)S(1)} %get-tuple-element.116), channel_id=1, source_target_pairs={{32,48},{33,57},{34,50},{35,59},{36,52},{37,61},{38,54},{39,63},{4... | collective-permute-start | bytes 1179656 | tf_op jit(solution)/shard_map/ppermute | solution.py:391
  89.0 1.4 collective-permute-start.6
  89.7 2.7 collective-permute-start.9
  91.7 1.4 collective-permute-start.8
  92.5 2.5 collective-permute-start.11
  94.2 7.2 %collective-permute-start.10 = (bf16[64,3072]{1,0:T(8,128)(2,1)S(1)}, bf16[64,3072]{1,0:T(8,128)(2,1)S(1)}, u32[]{:S(2)}, u32[]{:S(2)}) collective-permute-start(bf16[64,3072]{1,0:T(8,128)(2,1)S(1)} %get-tuple-element.127), channel_id=1, source_target_pairs={{64,80},{65,89},{66,82},{67,91},{68,84},{69,93},{70,86},{71,95},{7... | collective-permute-start | bytes 1179656 | tf_op jit(solution)/shard_map/ppermute | solution.py:391
  100.7 2.6 collective-permute-start.13
  102.6 7.0 %collective-permute-start.12 = (bf16[64,3072]{1,0:T(8,128)(2,1)S(1)}, bf16[64,3072]{1,0:T(8,128)(2,1)S(1)}, u32[]{:S(2)}, u32[]{:S(2)}) collective-permute-start(bf16[64,3072]{1,0:T(8,128)(2,1)S(1)} %get-tuple-element.133), channel_id=1, source_target_pairs={{80,96},{81,97},{82,98},{83,99},{84,100},{85,101},{86,102},{87,103... | collective-permute-start | bytes 1179656 | tf_op jit(solution)/shard_map/ppermute | solution.py:391
  104.5 6.9 %collective-permute-start.17 = (bf16[64,3072]{1,0:T(8,128)(2,1)S(1)}, bf16[64,3072]{1,0:T(8,128)(2,1)S(1)}, u32[]{:S(2)}, u32[]{:S(2)}) collective-permute-start(bf16[64,3072]{1,0:T(8,128)(2,1)S(1)} %get-tuple-element.144), channel_id=1, source_target_pairs={{96,112},{97,121},{98,114},{99,123},{100,116},{101,125},{102,118},... | collective-permute-start | bytes 1179656 | tf_op jit(solution)/shard_map/ppermute | solution.py:391
  105.1 4.5 copy-start.4
  108.9 3.2 collective-permute-start.16
  110.6 9.9 %collective-permute-start.15 = (bf16[64,3072]{1,0:T(8,128)(2,1)S(1)}, bf16[64,3072]{1,0:T(8,128)(2,1)S(1)}, u32[]{:S(2)}, u32[]{:S(2)}) collective-permute-start(bf16[64,3072]{1,0:T(8,128)(2,1)S(1)} %get-tuple-element.142), channel_id=1, source_target_pairs={{96,112},{97,121},{98,114},{99,123},{100,116},{101,125},{102,118},... | collective-permute-start | bytes 1179656 | tf_op jit(solution)/shard_map/ppermute | solution.py:391
  121.3 102.7 %collective-permute-start.22 = (bf16[256,3072]{1,0:T(8,128)(2,1)S(1)}, bf16[256,3072]{1,0:T(8,128)(2,1)S(1)}, u32[]{:S(2)}, u32[]{:S(2)}) collective-permute-start(bf16[256,3072]{1,0:T(8,128)(2,1)S(1)} %get-tuple-element.159.refs_0_), channel_id=1, source_target_pairs={{8,0},{9,1},{10,2},{11,3},{12,4},{13,5},{14,6},{15,7},{0,8},{1,9},... | collective-permute-start | bytes 4718600 | tf_op jit(solution)/shard_map/ppermute | solution.py:370
  186.8 1.4 collective-permute-start.14
  187.4 1.4 collective-permute-start.19
  188.2 1.4 collective-permute-start.18
  188.9 11.6 %collective-permute-start.21 = (bf16[64,3072]{1,0:T(8,128)(2,1)S(1)}, bf16[64,3072]{1,0:T(8,128)(2,1)S(1)}, u32[]{:S(2)}, u32[]{:S(2)}) collective-permute-start(bf16[64,3072]{1,0:T(8,128)(2,1)S(1)} %get-tuple-element.156), channel_id=1, source_target_pairs={{80,64},{89,65},{82,66},{91,67},{84,68},{93,69},{86,70},{95,71},{8... | collective-permute-start | bytes 1179656 | tf_op jit(solution)/shard_map/ppermute | solution.py:402
  198.2 2.3 collective-permute-start.20
  198.9 119.4 %collective-permute-start.29 = (bf16[256,3072]{1,0:T(8,128)(2,1)S(1)}, bf16[256,3072]{1,0:T(8,128)(2,1)}, u32[]{:S(2)}, u32[]{:S(2)}) collective-permute-start(bf16[256,3072]{1,0:T(8,128)(2,1)S(1)} %get-tuple-element.159.refs_0_), channel_id=1, source_target_pairs={{6,0},{7,1},{0,2},{1,3},{2,4},{3,5},{4,6},{5,7},{14,8},{15,9},{8,1... | collective-permute-start | bytes 4718600 | tf_op jit(solution)/shard_map/ppermute | solution.py:370
  224.1 101.3 %collective-permute-start.30 = (bf16[256,3072]{1,0:T(8,128)(2,1)S(1)}, bf16[256,3072]{1,0:T(8,128)(2,1)}, u32[]{:S(2)}, u32[]{:S(2)}) collective-permute-start(bf16[256,3072]{1,0:T(8,128)(2,1)S(1)} %get-tuple-element.172.refs_3_), channel_id=1, source_target_pairs={{2,0},{3,1},{4,2},{5,3},{6,4},{7,5},{0,6},{1,7},{10,8},{11,9},{12,... | collective-permute-start | bytes 4718600 | tf_op jit(solution)/shard_map/ppermute | solution.py:370
  226.9 1.4 collective-permute-start.24
  227.6 1.4 collective-permute-start.23
  228.4 9.8 %collective-permute-start.26 = (bf16[64,3072]{1,0:T(8,128)(2,1)S(1)}, bf16[64,3072]{1,0:T(8,128)(2,1)S(1)}, u32[]{:S(2)}, u32[]{:S(2)}) collective-permute-start(bf16[64,3072]{1,0:T(8,128)(2,1)S(1)} %get-tuple-element.165), channel_id=1, source_target_pairs={{48,32},{57,33},{50,34},{59,35},{52,36},{61,37},{54,38},{63,39},{5... | collective-permute-start | bytes 1179656 | tf_op jit(solution)/shard_map/ppermute | solution.py:402
  237.5 2.0 collective-permute-start.25
  238.2 73.8 %collective-permute-start.28 = (bf16[64,3072]{1,0:T(8,128)(2,1)S(1)}, bf16[64,3072]{1,0:T(8,128)(2,1)S(1)}, u32[]{:S(2)}, u32[]{:S(2)}) collective-permute-start(bf16[64,3072]{1,0:T(8,128)(2,1)S(1)} %get-tuple-element.169), channel_id=1, source_target_pairs={{32,16},{33,17},{34,18},{35,19},{36,20},{37,21},{38,22},{39,23},{4... | collective-permute-start | bytes 1179656 | tf_op jit(solution)/shard_map/ppermute | solution.py:402
  239.6 85.8 %collective-permute-start.27 = (bf16[64,3072]{1,0:T(8,128)(2,1)S(1)}, bf16[64,3072]{1,0:T(8,128)(2,1)S(1)}, u32[]{:S(2)}, u32[]{:S(2)}) collective-permute-start(bf16[64,3072]{1,0:T(8,128)(2,1)S(1)} %get-tuple-element.168), channel_id=1, source_target_pairs={{32,16},{33,17},{34,18},{35,19},{36,20},{37,21},{38,22},{39,23},{4... | collective-permute-start | bytes 1179656 | tf_op jit(solution)/shard_map/ppermute | solution.py:402
  316.4 19.1 %collective-permute-start.32 = (bf16[64,3072]{1,0:T(8,128)(2,1)S(1)}, bf16[64,3072]{1,0:T(8,128)(2,1)S(1)}, u32[]{:S(2)}, u32[]{:S(2)}) collective-permute-start(bf16[64,3072]{1,0:T(8,128)(2,1)S(1)} %get-tuple-element.174), channel_id=1, source_target_pairs={{16,0},{25,1},{18,2},{27,3},{20,4},{29,5},{22,6},{31,7},{24,8},{17... | collective-permute-start | bytes 1179656 | tf_op jit(solution)/shard_map/ppermute | solution.py:402
  333.6 12.3 %collective-permute-start.31 = (bf16[64,3072]{1,0:T(8,128)(2,1)S(1)}, bf16[64,3072]{1,0:T(8,128)(2,1)S(1)}, u32[]{:S(2)}, u32[]{:S(2)}) collective-permute-start(bf16[64,3072]{1,0:T(8,128)(2,1)S(1)} %get-tuple-element.173), channel_id=1, source_target_pairs={{16,0},{25,1},{18,2},{27,3},{20,4},{29,5},{22,6},{31,7},{24,8},{17... | collective-permute-start | bytes 1179656 | tf_op jit(solution)/shard_map/ppermute | solution.py:402
  339.9 13.8 %collective-permute-start.34 = (bf16[64,3072]{1,0:T(8,128)(2,1)S(1)}, bf16[64,3072]{1,0:T(8,128)(2,1)S(1)}, u32[]{:S(2)}, u32[]{:S(2)}) collective-permute-start(bf16[64,3072]{1,0:T(8,128)(2,1)S(1)} %get-tuple-element.178), channel_id=1, source_target_pairs={{16,0},{25,1},{18,2},{27,3},{20,4},{29,5},{22,6},{31,7},{24,8},{17... | collective-permute-start | bytes 1179656 | tf_op jit(solution)/shard_map/ppermute | solution.py:402
  350.3 17.1 %collective-permute-start.33 = (bf16[64,3072]{1,0:T(8,128)(2,1)S(1)}, bf16[64,3072]{1,0:T(8,128)(2,1)S(1)}, u32[]{:S(2)}, u32[]{:S(2)}) collective-permute-start(bf16[64,3072]{1,0:T(8,128)(2,1)S(1)} %get-tuple-element.177), channel_id=1, source_target_pairs={{16,0},{25,1},{18,2},{27,3},{20,4},{29,5},{22,6},{31,7},{24,8},{17... | collective-permute-start | bytes 1179656 | tf_op jit(solution)/shard_map/ppermute | solution.py:402
  351.6 37.5 %collective-permute-start.35 = (bf16[256,3072]{1,0:T(8,128)(2,1)S(1)}, bf16[256,3072]{1,0:T(8,128)(2,1)}, u32[]{:S(2)}, u32[]{:S(2)}) collective-permute-start(bf16[256,3072]{1,0:T(8,128)(2,1)S(1)} %get-tuple-element.159.refs_0_), channel_id=1, source_target_pairs={{2,0},{3,1},{4,2},{5,3},{6,4},{7,5},{0,6},{1,7},{10,8},{11,9},{12,... | collective-permute-start | bytes 4718600 | tf_op jit(solution)/shard_map/ppermute | solution.py:370
  352.4 38.6 %collective-permute-start.36 = (bf16[256,3072]{1,0:T(8,128)(2,1)S(1)}, bf16[256,3072]{1,0:T(8,128)(2,1)}, u32[]{:S(2)}, u32[]{:S(2)}) collective-permute-start(bf16[256,3072]{1,0:T(8,128)(2,1)S(1)} %get-tuple-element.172.refs_3_), channel_id=1, source_target_pairs={{6,0},{7,1},{0,2},{1,3},{2,4},{3,5},{4,6},{5,7},{14,8},{15,9},{8,1... | collective-permute-start | bytes 4718600 | tf_op jit(solution)/shard_map/ppermute | solution.py:370
  353.7 79.5 %collective-permute-start.37 = (bf16[256,3072]{1,0:T(8,128)(2,1)}, bf16[256,3072]{1,0:T(8,128)(2,1)}, u32[]{:S(2)}, u32[]{:S(2)}) collective-permute-start(bf16[256,3072]{1,0:T(8,128)(2,1)} %get-tuple-element.182.refs_1_), channel_id=1, source_target_pairs={{6,0},{7,1},{0,2},{1,3},{2,4},{3,5},{4,6},{5,7},{14,8},{15,9},{8,1... | collective-permute-start | bytes 4718600 | tf_op jit(solution)/shard_map/ppermute | solution.py:370
  353.7 79.5 %collective-permute-start.38 = (bf16[256,3072]{1,0:T(8,128)(2,1)}, bf16[256,3072]{1,0:T(8,128)(2,1)}, u32[]{:S(2)}, u32[]{:S(2)}) collective-permute-start(bf16[256,3072]{1,0:T(8,128)(2,1)} %get-tuple-element.183.refs_5_), channel_id=1, source_target_pairs={{2,0},{3,1},{4,2},{5,3},{6,4},{7,5},{0,6},{1,7},{10,8},{11,9},{12,... | collective-permute-start | bytes 4718600 | tf_op jit(solution)/shard_map/ppermute | solution.py:370
  368.2 1.2 copy-start.6
  369.4 66.7 %all-to-all-start = ((bf16[8,384,256]{2,1,0:T(8,128)(2,1)}), bf16[8,384,256]{2,1,0:T(8,128)(2,1)}, u32[]{:S(2)}, u32[]{:S(2)}) async-start(bf16[8,384,256]{2,1,0:T(8,128)(2,1)} %copy-done.6), calls=%async_computation | async-start | bytes 3145728 | tf_op jit(solution)/shard_map/all_to_all | solution.py:417
  445.5 2.9 collective-permute-start.39
  449.7 24.9 %all-to-all-start.1 = ((bf16[8,192,384]{2,1,0:T(8,128)(2,1)}), bf16[8,192,384]{2,1,0:T(8,128)(2,1)S(1)}, u32[]{:S(2)}, u32[]{:S(2)}) async-start(bf16[8,192,384]{2,1,0:T(8,128)(2,1)} %add_cores.1), calls=%async_computation.1 | async-start | bytes 2359296 | tf_op jit(solution)/shard_map/all_to_all | solution.py:421
  (1 other events, 1.1 us)
